TPU v7x, 32 devices: a whole 2x2x4 slice. The times are simulated.
32 devices in a mesh: exc: 2 (over core), line: 16 (over z, y, x).
Axes of the slice: x: 2, y: 2, z: 4, core: 2. Of those that a mesh axis runs over, the one named last changes fastest.
Arguments:
- adj_e: float32 [3, 2, 1024, 1024], P(None, 'exc', 'line'), parts along dimension 1, may hold values from -6 to 6
- adj_h: float32 [3, 2, 1024, 1024], P(None, 'exc', 'line'), parts along dimension 1, may hold values from -6 to 6
- fwd_e: bfloat16 [2, 3, 2, 1024, 1024], P(None, None, 'exc', 'line'), parts along dimension 2, may hold values from -6 to 6
- permittivity: float32 [1, 1024, 1024], P(None, 'line'), may hold values from 1 to 6
- design_mask: int32 [1, 1024, 1024], P(None, 'line'), may hold values 0 or 1
- inverse: bfloat16 [1024, 1024], replicated, may hold values from -0.03125 to 0.6875
- omega: float32 [2], P('exc'), parts along dimension 0, may hold values from 0.3 to 2.5
- port_mode: float32 [2048], P('exc'), parts along dimension 0, may hold values from -6 to 6
- port_plane: int32 [2], P('exc'), parts along dimension 0, may hold values from 0 to 1023
Outputs:
- adj_e_out: float32 [3, 2, 1024, 1024], P(None, 'exc', 'line'), parts along dimension 1
- adj_h_out: float32 [3, 2, 1024, 1024], P(None, 'exc', 'line'), parts along dimension 1
- gradient: float32 [2, 1024, 1024], P('exc', 'line'), parts along dimension 0
There are 2 independent parts, one for each index of `exc`. A program takes and returns all parts, laid end to end along the dimension named above; an argument that names none is the same for every part. Nothing has to cross between parts.
All inputs are finite; a program needn't handle non-finite values. No bound on the sum of `design_mask` on one device may be relied on, other than what follows from the above.
Results may differ from a plain program's by a relative error of at most 0.005.
Values may be sent and summed in bfloat16 or wider, within the bound.
A program may use at most 64 MiB of HBM per device.

v0:
```python
import jax
import jax.numpy as jnp
from jax import lax
from jax.sharding import PartitionSpec as P

COURANT = 0.4


def extended(array, sides, width):
    for axis, dim in sides:
        devices, length = (lax.axis_size(axis), array.shape[dim])
        up = [(i, (i + 1) % devices) for i in range(devices - 1)]
        down = [(j, i) for i, j in up]
        last = lax.slice_in_dim(array, length - width, length, axis=dim)
        first = lax.slice_in_dim(array, 0, width, axis=dim)
        before = lax.ppermute(last, axis, up)
        after = lax.ppermute(first, axis, down)
        array = jnp.concatenate([before, array, after], axis=dim)
    return array


def lower_diff(padded, along):
    inner = padded.shape[along] - 2
    middle = lax.slice_in_dim(padded, 1, inner + 1, axis=along)
    return middle - lax.slice_in_dim(padded, 0, inner, axis=along)


def upper_diff(padded, along):
    inner = padded.shape[along] - 2
    middle = lax.slice_in_dim(padded, 1, inner + 1, axis=along)
    return lax.slice_in_dim(padded, 2, inner + 2, axis=along) - middle


def zero_rim(stacked, along):
    widths = [(0, 0)] * stacked.ndim
    widths[along] = (1, 1)
    return jnp.pad(stacked, widths)


def row_rim(stacked, along):
    return extended(stacked, (("line", 2),), 1)


def column_rim(stacked, along):
    return extended(stacked, (("line", 2),), 1)


def curl_along_y(fields, inverse_eps, extend, along):
    electric_x, electric_y, electric_z = (fields[0], fields[1], fields[2])
    magnetic_x, magnetic_y, magnetic_z = (fields[3], fields[4], fields[5])
    scaled = COURANT * inverse_eps
    lower_terms = lower_diff(extend(jnp.stack([magnetic_x, magnetic_z]), along), along)
    electric_x = electric_x + scaled * lower_terms[1]
    electric_z = electric_z - scaled * lower_terms[0]
    upper_terms = upper_diff(extend(jnp.stack([electric_x, electric_z]), along), along)
    magnetic_x = magnetic_x - COURANT * upper_terms[1]
    magnetic_z = magnetic_z + COURANT * upper_terms[0]
    return jnp.stack([electric_x, electric_y, electric_z, magnetic_x, magnetic_y, magnetic_z])


def curl_along_xz(fields, inverse_eps, extend, along):
    electric_x, electric_y, electric_z = (fields[0], fields[1], fields[2])
    magnetic_x, magnetic_y, magnetic_z = (fields[3], fields[4], fields[5])
    scaled = COURANT * inverse_eps
    depth_terms = lower_diff(zero_rim(jnp.stack([magnetic_x, magnetic_y]), 1), 1)
    across = lower_diff(extend(jnp.stack([magnetic_y, magnetic_z]), along), along)
    electric_x = electric_x - scaled * depth_terms[1]
    electric_y = electric_y + scaled * (depth_terms[0] - across[1])
    electric_z = electric_z + scaled * across[0]
    depth_upper = upper_diff(zero_rim(jnp.stack([electric_x, electric_y]), 1), 1)
    across_upper = upper_diff(extend(jnp.stack([electric_y, electric_z]), along), along)
    magnetic_x = magnetic_x + COURANT * depth_upper[1]
    magnetic_y = magnetic_y + COURANT * (across_upper[1] - depth_upper[0])
    magnetic_z = magnetic_z - COURANT * across_upper[0]
    return jnp.stack([electric_x, electric_y, electric_z, magnetic_x, magnetic_y, magnetic_z])


def line_solve(rounded, inverse):
    flattened = rounded.reshape(-1, rounded.shape[-1])
    solved = lax.dot_general(
        flattened, inverse, (((1,), (1,)), ((), ())), preferred_element_type=jnp.float32
    )
    return solved.reshape(rounded.shape)


def fold_lines(field, line_count):
    strip_width = field.shape[-2]
    block = field.shape[-1] // line_count
    regrouped = field.reshape(field.shape[:-2] + (strip_width, line_count, block))
    regrouped = jnp.moveaxis(regrouped, -3, -1)
    return regrouped.reshape(field.shape[:-2] + (line_count, block * strip_width))


def unfold(received, block):
    line_count = received.shape[-2]
    strip_width = received.shape[-1] // block
    regrouped = received.reshape(received.shape[:-2] + (line_count, block, strip_width))
    regrouped = jnp.moveaxis(regrouped, -3, -2)
    return regrouped.reshape(received.shape[:-2] + (block, line_count * strip_width))


def accumulate(gradient, fields, snapshot, mask_weight, inverse_cols):
    forward = snapshot.astype(jnp.float32)
    intersection = fields[0] * forward[0] + fields[1] * forward[1] + fields[2] * forward[2]
    return gradient + mask_weight * intersection * (inverse_cols * inverse_cols)


def per_device(
    adj_e, adj_h, fwd_e, permittivity, design_mask, inverse, omega, port_mode, port_plane
):
    line_cells = inverse.shape[0]
    strip_width = adj_e.shape[2]
    step_count = fwd_e.shape[0]
    line_count = lax.axis_size("line")
    fields = jnp.concatenate([adj_e, adj_h], 0)
    inverse_rows = 1.0 / permittivity
    eps_turned = lax.all_to_all(
        fold_lines(permittivity, line_count), "line", split_axis=1, concat_axis=1, tiled=True
    )
    inverse_cols = 1.0 / unfold(eps_turned, strip_width)
    frequency = omega[0]
    plane_at = port_plane[0]
    offset = lax.axis_index("line") * strip_width
    column = (jnp.arange(line_cells, dtype=jnp.int32) == plane_at).astype(jnp.float32)
    profile_rows = lax.dynamic_slice_in_dim(port_mode, offset, strip_width)
    mask_weight = design_mask.astype(jnp.float32)
    gradient = jnp.zeros(permittivity.shape, jnp.float32)
    for instant in range(step_count):
        amplitude = jnp.cos(frequency * (instant + 1))
        fields = fields.at[2].add(amplitude * profile_rows[None, :, None] * column[None, None, :])
        fields = curl_along_y(fields, inverse_rows, row_rim, 2)
        fields = line_solve(fields.astype(jnp.bfloat16), inverse)
        turned = unfold(
            lax.all_to_all(
                fold_lines(fields, line_count), "line", split_axis=2, concat_axis=2, tiled=True
            ),
            strip_width,
        )
        turned = curl_along_xz(turned, inverse_cols, column_rim, 2)
        turned = line_solve(turned.astype(jnp.bfloat16), inverse)
        gradient = accumulate(gradient, turned, fwd_e[instant], mask_weight, inverse_cols)
        if instant + 1 < step_count:
            fields = unfold(
                lax.all_to_all(
                    fold_lines(turned, line_count), "line", split_axis=2, concat_axis=2, tiled=True
                ),
                strip_width,
            )
    return (turned[:3], turned[3:], gradient)


def solution(mesh):
    in_specs = (
        P(None, "exc", "line", None),
        P(None, "exc", "line", None),
        P(None, None, "exc", "line", None),
        P(None, "line", None),
        P(None, "line", None),
        P(),
        P("exc"),
        P("exc"),
        P("exc"),
    )
    out_specs = (P(None, "exc", "line", None), P(None, "exc", "line", None), P("exc", "line", None))
    return jax.shard_map(
        per_device, mesh=mesh, in_specs=in_specs, out_specs=out_specs, check_vma=False
    )
```

profile of v0, /device:TPU:0, one launch (start us, length us, event | category | flops | bytes accessed | tf_op | source)
XLA Modules:
  0.0 337.1 jit_solution(8873413858558898854)
XLA Ops:
  1.9 4.8 %collective-permute-start = (f32[2,1,1,1024]{3,2,1,0:T(1,128)S(1)}, f32[2,1,1,1024]{3,2,1,0:T(1,128)S(1)}, u32[]{:S(2)}, u32[]{:S(2)}) collective-permute-start(f32[2,1,1,1024]{3,2,1,0:T(1,128)S(1)} %fusion.84), channel_id=1, source_target_pairs={{0,1},{1,2},{2,3},{3,4},{4,5},{5,6},{6,7},{7,8},{8,9},{9,10},{10,1... | collective-permute-start | bytes 24584 | tf_op jit(solution)/shard_map/ppermute | solution.py:16
  13.8 8.7 %all-to-all-start.1 = ((f32[1,16,4096]{2,0,1:T(1,128)}), f32[1,16,4096]{2,0,1:T(1,128)S(1)}, u32[]{:S(2)}, u32[]{:S(2)}) async-start(f32[1,16,4096]{2,0,1:T(1,128)} %reshape.867), calls=%async_computation.1 | async-start | bytes 524288 | tf_op jit(solution)/shard_map/all_to_all | solution.py:117
  27.5 4.6 %convolution_bitcast_fusion.1 = f32[6,1,16,64,64]{3,4,2,0,1:T(8,128)} fusion(bf16[16,64,1024,1]{2,1,0,3:T(8,128)(2,1)S(1)} %bitcast.258, bf16[6,64,1024]{2,1,0:T(8,128)(2,1)} %fusion.69), kind=kOutput, calls=%fused_computation.1 | convolution fusion | flops 805306368 | bytes 4456448 | tf_op jit(solution)/shard_map/dot_general | solution.py:80
  32.1 3.5 %copy.123 = f32[6,1,16,64,64]{4,3,0,2,1:T(8,128)} copy(f32[6,1,16,64,64]{3,4,2,0,1:T(8,128)} %convolution_bitcast_fusion.1) | data formatting | bytes 3145728 | tf_op jit(solution)/shard_map/reshape | solution.py:91
  35.6 4.5 %reshape.866 = f32[6,1,16,4096]{3,1,0,2:T(1,128)} reshape(f32[6,1,16,64,64]{4,3,0,2,1:T(8,128)} %copy.123) | data formatting | bytes 3145728 | tf_op jit(solution)/shard_map/reshape | solution.py:91
  40.1 7.0 %all-to-all-start = ((f32[6,1,16,4096]{3,1,0,2:T(1,128)}), f32[6,1,16,4096]{3,1,0,2:T(1,128)}, u32[]{:S(2)}, u32[]{:S(2)}) async-start(f32[6,1,16,4096]{3,1,0,2:T(1,128)} %reshape.866), calls=%async_computation | async-start | bytes 3145728 | tf_op jit(solution)/shard_map/all_to_all | solution.py:134
  52.1 27.6 %all-to-all-done = f32[6,1,16,4096]{3,1,0,2:T(1,128)} async-done(((f32[6,1,16,4096]{3,1,0,2:T(1,128)}), f32[6,1,16,4096]{3,1,0,2:T(1,128)}, u32[]{:S(2)}, u32[]{:S(2)}) %all-to-all-start) | async-done | bytes 1572896 | tf_op jit(solution)/shard_map/all_to_all | solution.py:134
  79.7 3.7 %copy.85 = f32[6,1,16,4096]{3,2,0,1:T(8,128)} copy(f32[6,1,16,4096]{3,1,0,2:T(1,128)} %all-to-all-done) | data formatting | bytes 3145728 | tf_op jit(solution)/shard_map/all_to_all | solution.py:134
  83.4 3.5 %reshape.854 = f32[6,1,16,64,64]{4,3,2,0,1:T(8,128)} reshape(f32[6,1,16,4096]{3,2,0,1:T(8,128)} %copy.85) | data formatting | bytes 3145728 | tf_op jit(solution)/shard_map/reshape | solution.py:97
  124.7 5.6 %collective-permute-done.3 = f32[2,1,1,1024]{3,2,1,0:T(1,128)S(1)} collective-permute-done((f32[2,1,1,1024]{3,2,1,0:T(1,128)S(1)}, f32[2,1,1,1024]{3,2,1,0:T(1,128)S(1)}, u32[]{:S(2)}, u32[]{:S(2)}) %collective-permute-start.3) | collective-permute-done | bytes 8224 | tf_op jit(solution)/shard_map/ppermute | solution.py:17
  132.9 3.4 %reshape_reshape.2 = f32[6,1,64,16,64]{4,3,2,0,1:T(8,128)} reshape(f32[384,1024]{1,0:T(8,128)} %fusion.100) | data formatting | bytes 3145728 | tf_op jit(solution)/shard_map/reshape;reshape | solution.py:89
  136.3 3.7 %copy.98 = f32[6,1,64,16,64]{2,4,3,0,1:T(8,128)} copy(f32[6,1,64,16,64]{4,3,2,0,1:T(8,128)} %reshape_reshape.2) | data formatting | bytes 3145728 | tf_op jit(solution)/shard_map/reshape;reshape | solution.py:89
  146.3 42.7 %all_to_all.20 = f32[6,1,16,4096]{3,1,0,2:T(1,128)S(1)} all-to-all(f32[6,1,16,4096]{3,1,0,2:T(1,128)S(1)} %copy.99), channel_id=1, replica_groups=mesh['exc'=2,'line'=16] {'line'}, dimensions={2} | all-to-all | bytes 3145728 | tf_op jit(solution)/shard_map/all_to_all | solution.py:144
  191.3 3.5 %reshape.858 = f32[6,1,16,64,64]{4,3,2,0,1:T(8,128)} reshape(f32[6,1,16,4096]{3,2,0,1:T(8,128)} %copy.100) | data formatting | bytes 3145728 | tf_op jit(solution)/shard_map/reshape | solution.py:97
  194.8 3.6 %bitcast_convert_fusion = bf16[6,1,64,16,64]{4,2,3,0,1:T(8,128)(2,1)} fusion(f32[6,1,16,64,64]{4,3,2,0,1:T(8,128)} %reshape.858), kind=kLoop, calls=%fused_computation.173 | loop fusion | flops 393216 | bytes 2359296 | tf_op jit(solution)/shard_map/convert.17
  226.7 3.8 %collective-permute-done.5 = f32[2,1,1,1024]{3,2,1,0:T(1,128)S(1)} collective-permute-done((f32[2,1,1,1024]{3,2,1,0:T(1,128)S(1)}, f32[2,1,1,1024]{3,2,1,0:T(1,128)S(1)}, u32[]{:S(2)}, u32[]{:S(2)}) %collective-permute-start.5) | collective-permute-done | bytes 8224 | tf_op jit(solution)/shard_map/ppermute | solution.py:17
  233.7 4.6 %convolution_bitcast_fusion = f32[6,1,16,64,64]{3,4,2,0,1:T(8,128)} fusion(bf16[16,64,1024,1]{2,1,0,3:T(8,128)(2,1)S(1)} %bitcast.259, bf16[6,64,1024]{2,1,0:T(8,128)(2,1)} %fusion.76), kind=kOutput, calls=%fused_computation | convolution fusion | flops 805306368 | bytes 4456448 | tf_op jit(solution)/shard_map/dot_general | solution.py:80
  238.4 3.5 %copy.125 = f32[6,1,16,64,64]{4,3,0,2,1:T(8,128)} copy(f32[6,1,16,64,64]{3,4,2,0,1:T(8,128)} %convolution_bitcast_fusion) | data formatting | bytes 3145728 | tf_op jit(solution)/shard_map/reshape | solution.py:91
  241.9 4.5 %reshape.868 = f32[6,1,16,4096]{3,1,0,2:T(1,128)} reshape(f32[6,1,16,64,64]{4,3,0,2,1:T(8,128)} %copy.125) | data formatting | bytes 3145728 | tf_op jit(solution)/shard_map/reshape | solution.py:91
  246.3 7.0 %all-to-all-start.3 = ((f32[6,1,16,4096]{3,1,0,2:T(1,128)}), f32[6,1,16,4096]{3,1,0,2:T(1,128)}, u32[]{:S(2)}, u32[]{:S(2)}) async-start(f32[6,1,16,4096]{3,1,0,2:T(1,128)} %reshape.868), calls=%async_computation.3 | async-start | bytes 3145728 | tf_op jit(solution)/shard_map/all_to_all | solution.py:134
  258.0 26.2 %all-to-all-done.3 = f32[6,1,16,4096]{3,1,0,2:T(1,128)} async-done(((f32[6,1,16,4096]{3,1,0,2:T(1,128)}), f32[6,1,16,4096]{3,1,0,2:T(1,128)}, u32[]{:S(2)}, u32[]{:S(2)}) %all-to-all-start.3) | async-done | bytes 1572896 | tf_op jit(solution)/shard_map/all_to_all | solution.py:134
  284.1 3.7 %copy.109 = f32[6,1,16,4096]{3,2,0,1:T(8,128)} copy(f32[6,1,16,4096]{3,1,0,2:T(1,128)} %all-to-all-done.3) | data formatting | bytes 3145728 | tf_op jit(solution)/shard_map/all_to_all | solution.py:134
  287.8 3.5 %reshape.861 = f32[6,1,16,64,64]{4,3,2,0,1:T(8,128)} reshape(f32[6,1,16,4096]{3,2,0,1:T(8,128)} %copy.109) | data formatting | bytes 3145728 | tf_op jit(solution)/shard_map/reshape | solution.py:97
  326.6 5.7 %collective-permute-done.7 = f32[2,1,1,1024]{3,2,1,0:T(1,128)S(1)} collective-permute-done((f32[2,1,1,1024]{3,2,1,0:T(1,128)S(1)}, f32[2,1,1,1024]{3,2,1,0:T(1,128)S(1)}, u32[]{:S(2)}, u32[]{:S(2)}) %collective-permute-start.7) | collective-permute-done | bytes 8224 | tf_op jit(solution)/shard_map/ppermute | solution.py:17
  (184 shorter events, 141.4 us)
Async XLA Ops:
  0.6 26.9 %copy-start = (bf16[1024,1024]{1,0:T(8,128)(2,1)S(1)}, bf16[1024,1024]{1,0:T(8,128)(2,1)}, u32[]{:S(2)}) copy-start(bf16[1024,1024]{1,0:T(8,128)(2,1)} %param.18) | copy-start | bytes 6291460
  0.6 8.5 %copy-start.2 = (f32[1,64,1024]{2,1,0:T(8,128)S(1)}, f32[1,64,1024]{2,1,0:T(8,128)}, u32[]{:S(2)}) copy-start(f32[1,64,1024]{2,1,0:T(8,128)} %param.16) | copy-start | bytes 786436
  1.9 7.2 %collective-permute-start = (f32[2,1,1,1024]{3,2,1,0:T(1,128)S(1)}, f32[2,1,1,1024]{3,2,1,0:T(1,128)S(1)}, u32[]{:S(2)}, u32[]{:S(2)}) collective-permute-start(f32[2,1,1,1024]{3,2,1,0:T(1,128)S(1)} %fusion.84), channel_id=1, source_target_pairs={{0,1},{1,2},{2,3},{3,4},{4,5},{5,6},{6,7},{7,8},{8,9},{9,10},{10,1... | collective-permute-start | bytes 24584 | tf_op jit(solution)/shard_map/ppermute | solution.py:16
  11.2 11.3 %collective-permute-start.1 = (f32[2,1,1,1024]{3,2,1,0:T(1,128)S(1)}, f32[2,1,1,1024]{3,2,1,0:T(1,128)S(1)}, u32[]{:S(2)}, u32[]{:S(2)}) collective-permute-start(f32[2,1,1,1024]{3,2,1,0:T(1,128)S(1)} %fusion.83), channel_id=1, source_target_pairs={{1,0},{2,1},{3,2},{4,3},{5,4},{6,5},{7,6},{8,7},{9,8},{10,9},{11,1... | collective-permute-start | bytes 24584 | tf_op jit(solution)/shard_map/ppermute | solution.py:17
  13.8 26.3 %all-to-all-start.1 = ((f32[1,16,4096]{2,0,1:T(1,128)}), f32[1,16,4096]{2,0,1:T(1,128)S(1)}, u32[]{:S(2)}, u32[]{:S(2)}) async-start(f32[1,16,4096]{2,0,1:T(1,128)} %reshape.867), calls=%async_computation.1 | async-start | bytes 524288 | tf_op jit(solution)/shard_map/all_to_all | solution.py:117
  40.1 39.6 %all-to-all-start = ((f32[6,1,16,4096]{3,1,0,2:T(1,128)}), f32[6,1,16,4096]{3,1,0,2:T(1,128)}, u32[]{:S(2)}, u32[]{:S(2)}) async-start(f32[6,1,16,4096]{3,1,0,2:T(1,128)} %reshape.866), calls=%async_computation | async-start | bytes 3145728 | tf_op jit(solution)/shard_map/all_to_all | solution.py:134
  100.0 19.4 %collective-permute-start.2 = (f32[2,1,1,1024]{3,2,1,0:T(1,128)S(1)}, f32[2,1,1,1024]{3,2,1,0:T(1,128)S(1)}, u32[]{:S(2)}, u32[]{:S(2)}) collective-permute-start(f32[2,1,1,1024]{3,2,1,0:T(1,128)S(1)} %slice.452), channel_id=1, source_target_pairs={{0,1},{1,2},{2,3},{3,4},{4,5},{5,6},{6,7},{7,8},{8,9},{9,10},{10,1... | collective-permute-start | bytes 24584 | tf_op jit(solution)/shard_map/ppermute | solution.py:16
  119.4 5.2 %copy-start.7 = (f32[1,64,1024]{2,1,0:T(8,128)S(1)}, f32[1,64,1024]{2,1,0:T(8,128)}, u32[]{:S(2)}) copy-start(f32[1,64,1024]{2,1,0:T(8,128)} %mul.346) | copy-start | bytes 786436
  119.4 5.2 %copy-start.15 = (f32[1,64,1024]{2,1,0:T(8,128)S(1)}, f32[1,64,1024]{2,1,0:T(8,128)}, u32[]{:S(2)}) copy-start(f32[1,64,1024]{2,1,0:T(8,128)} %squeeze.52) | copy-start | bytes 786436
  119.4 5.2 %copy-start.16 = (f32[1,64,1024]{2,1,0:T(8,128)S(1)}, f32[1,64,1024]{2,1,0:T(8,128)}, u32[]{:S(2)}) copy-start(f32[1,64,1024]{2,1,0:T(8,128)} %stack.128) | copy-start | bytes 786436
  123.2 7.3 %copy-start.24 = (bf16[6,1,64,1024]{3,2,1,0:T(8,128)(2,1)S(1)}, bf16[6,1,64,1024]{3,2,1,0:T(8,128)(2,1)}, u32[]{:S(2)}) copy-start(bf16[6,1,64,1024]{3,2,1,0:T(8,128)(2,1)} %get-tuple-element.47) | copy-start | bytes 2359300
  123.2 7.4 %copy-start.6 = (f32[1,1,64,1024]{3,2,1,0:T(8,128)S(1)}, f32[1,1,64,1024]{3,2,1,0:T(8,128)}, u32[]{:S(2)}) copy-start(f32[1,1,64,1024]{3,2,1,0:T(8,128)} %slice.373) | copy-start | bytes 786436
  123.2 7.1 %collective-permute-start.3 = (f32[2,1,1,1024]{3,2,1,0:T(1,128)S(1)}, f32[2,1,1,1024]{3,2,1,0:T(1,128)S(1)}, u32[]{:S(2)}, u32[]{:S(2)}) collective-permute-start(f32[2,1,1,1024]{3,2,1,0:T(1,128)S(1)} %fusion.82), channel_id=1, source_target_pairs={{1,0},{2,1},{3,2},{4,3},{5,4},{6,5},{7,6},{8,7},{9,8},{10,9},{11,1... | collective-permute-start | bytes 24584 | tf_op jit(solution)/shard_map/ppermute | solution.py:17
  208.1 14.9 %collective-permute-start.4 = (f32[2,1,1,1024]{3,2,1,0:T(1,128)}, f32[2,1,1,1024]{3,2,1,0:T(1,128)S(1)}, u32[]{:S(2)}, u32[]{:S(2)}) collective-permute-start(f32[2,1,1,1024]{3,2,1,0:T(1,128)} %slice.465), channel_id=1, source_target_pairs={{0,1},{1,2},{2,3},{3,4},{4,5},{5,6},{6,7},{7,8},{8,9},{9,10},{10,1... | collective-permute-start | bytes 24584 | tf_op jit(solution)/shard_map/ppermute | solution.py:16
  225.0 5.5 %collective-permute-start.5 = (f32[2,1,1,1024]{3,2,1,0:T(1,128)S(1)}, f32[2,1,1,1024]{3,2,1,0:T(1,128)S(1)}, u32[]{:S(2)}, u32[]{:S(2)}) collective-permute-start(f32[2,1,1,1024]{3,2,1,0:T(1,128)S(1)} %fusion.81), channel_id=1, source_target_pairs={{1,0},{2,1},{3,2},{4,3},{5,4},{6,5},{7,6},{8,7},{9,8},{10,9},{11,1... | collective-permute-start | bytes 24584 | tf_op jit(solution)/shard_map/ppermute | solution.py:17
  246.3 7.1 %copy-start.22 = (bf16[2,3,1,64,1024]{4,3,2,1,0:T(8,128)(2,1)S(1)}, bf16[2,3,1,64,1024]{4,3,2,1,0:T(8,128)(2,1)}, u32[]{:S(2)}) copy-start(bf16[2,3,1,64,1024]{4,3,2,1,0:T(8,128)(2,1)} %param.15) | copy-start | bytes 2359300
  246.3 8.4 %copy-start.12 = (f32[16,4096]{1,0:T(8,128)S(1)}, f32[16,4096]{1,0:T(8,128)}, u32[]{:S(2)}) copy-start(f32[16,4096]{1,0:T(8,128)} %get-tuple-element.39) | copy-start | bytes 786436
  246.3 37.8 %all-to-all-start.3 = ((f32[6,1,16,4096]{3,1,0,2:T(1,128)}), f32[6,1,16,4096]{3,1,0,2:T(1,128)}, u32[]{:S(2)}, u32[]{:S(2)}) async-start(f32[6,1,16,4096]{3,1,0,2:T(1,128)} %reshape.868), calls=%async_computation.3 | async-start | bytes 3145728 | tf_op jit(solution)/shard_map/all_to_all | solution.py:134
  302.8 18.5 %collective-permute-start.6 = (f32[2,1,1,1024]{3,2,1,0:T(1,128)S(1)}, f32[2,1,1,1024]{3,2,1,0:T(1,128)S(1)}, u32[]{:S(2)}, u32[]{:S(2)}) collective-permute-start(f32[2,1,1,1024]{3,2,1,0:T(1,128)S(1)} %slice.480), channel_id=1, source_target_pairs={{0,1},{1,2},{2,3},{3,4},{4,5},{5,6},{6,7},{7,8},{8,9},{9,10},{10,1... | collective-permute-start | bytes 24584 | tf_op jit(solution)/shard_map/ppermute | solution.py:16
  309.0 6.0 %copy-start.10 = (f32[1,1,64,16,64]{4,2,3,0,1:T(8,128)S(1)}, f32[1,1,64,16,64]{4,2,3,0,1:T(8,128)}, u32[]{:S(2)}) copy-start(f32[1,1,64,16,64]{4,2,3,0,1:T(8,128)} %get-tuple-element.55) | copy-start | bytes 786436
  321.3 5.2 %copy-start.13 = (f32[1,64,1024]{2,1,0:T(8,128)S(1)}, f32[1,64,1024]{2,1,0:T(8,128)}, u32[]{:S(2)}) copy-start(f32[1,64,1024]{2,1,0:T(8,128)} %squeeze.59) | copy-start | bytes 786436
  321.3 5.2 %copy-start.14 = (f32[1,64,1024]{2,1,0:T(8,128)S(1)}, f32[1,64,1024]{2,1,0:T(8,128)}, u32[]{:S(2)}) copy-start(f32[1,64,1024]{2,1,0:T(8,128)} %stack.145) | copy-start | bytes 786436
  325.1 7.3 %copy-start.25 = (bf16[6,1,64,1024]{3,2,1,0:T(8,128)(2,1)S(1)}, bf16[6,1,64,1024]{3,2,1,0:T(8,128)(2,1)}, u32[]{:S(2)}) copy-start(bf16[6,1,64,1024]{3,2,1,0:T(8,128)(2,1)} %get-tuple-element.41) | copy-start | bytes 2359300
  325.1 7.2 %collective-permute-start.7 = (f32[2,1,1,1024]{3,2,1,0:T(1,128)S(1)}, f32[2,1,1,1024]{3,2,1,0:T(1,128)S(1)}, u32[]{:S(2)}, u32[]{:S(2)}) collective-permute-start(f32[2,1,1,1024]{3,2,1,0:T(1,128)S(1)} %fusion.80), channel_id=1, source_target_pairs={{1,0},{2,1},{3,2},{4,3},{5,4},{6,5},{7,6},{8,7},{9,8},{10,9},{11,1... | collective-permute-start | bytes 24584 | tf_op jit(solution)/shard_map/ppermute | solution.py:17
  (15 other events, 34.9 us)
where the time goes:
time: 343 us; the launch traced here: 337 us
  local copies, waits for them, and re-layouts  141 us (41%)
  waiting for transfers between devices  68.9 us (20%)
  blocking collectives  42.7 us (12%)
  starting transfers between devices  41.1 us (12%)
  other arithmetic  28.4 us (8%)
  matrix products  12.5 us (4%)
    all_to_all x2, waiting for transfers between devices, per_device(): lax.all_to_all(fold_lines(fields, line_count), 'line', split_axis=2, conc...  53.8 us
    all_to_all x1, blocking collectives, per_device(): lax.all_to_all(fold_lines(turned, line_count), 'line', split_axis=2, conc...  42.7 us
    reshape x7, local copies, waits for them, and re-layouts, fold_lines(): regrouped.reshape(field.shape[:-2] + (line_count, block * strip_width))  23.3 us
    slice x8, local copies, waits for them, and re-layouts, curl_along_xz(): electric_x, electric_y, electric_z = (fields[0], fields[1], fields[2])  15.7 us
    ppermute x4, waiting for transfers between devices, extended(): after = lax.ppermute(first, axis, down)  15.1 us
    all_to_all x2, starting transfers between devices, per_device(): lax.all_to_all(fold_lines(fields, line_count), 'line', split_axis=2, conc...  14 us
    ppermute x4, starting transfers between devices, extended(): before = lax.ppermute(last, axis, up)  13 us
    slice x8, local copies, waits for them, and re-layouts, curl_along_xz(): magnetic_x, magnetic_y, magnetic_z = (fields[3], fields[4], fields[5])  12.8 us
  transfers between devices with their start and end apart: 11, of which 5 were waited for; matrix products, arithmetic and copies ran while one was open for 22% of the time, Pallas kernels for 0%

commit v1 on v0

--- a/solution.py
+++ b/solution.py
@@ -1,6 +1,10 @@
+import functools
+
 import jax
 import jax.numpy as jnp
 from jax import lax
+from jax.experimental import pallas as pl
+from jax.experimental.pallas import tpu as pltpu
 from jax.sharding import PartitionSpec as P
 
 COURANT = 0.4
@@ -105,7 +109,7 @@
     return gradient + mask_weight * intersection * (inverse_cols * inverse_cols)
 
 
-def per_device(
+def plain_per_device(
     adj_e, adj_h, fwd_e, permittivity, design_mask, inverse, omega, port_mode, port_plane
 ):
     line_cells = inverse.shape[0]
@@ -149,6 +153,342 @@
     return (turned[:3], turned[3:], gradient)
 
 
+LANES = 128
+MESH = pl.DeviceIdType.MESH
+PAD = 8
+F32, BF16 = (jnp.float32, jnp.bfloat16)
+PAIRS_X = ((0, 1), (2, 3), (4, 5))
+PAIRS_Y = ((0, 2), (1, 4), (5, 3))
+
+
+def contract(left, right):
+    return lax.dot_general(left, right, (((1,), (1,)), ((), ())), preferred_element_type=F32)
+
+
+def shifted_down(value, first):
+    row = lax.broadcasted_iota(jnp.int32, value.shape, 0)
+    return jnp.where(row == 0, first, pltpu.roll(value, 1, 0))
+
+
+def shifted_up(value, last):
+    rows = value.shape[0]
+    row = lax.broadcasted_iota(jnp.int32, value.shape, 0)
+    return jnp.where(row == rows - 1, last, pltpu.roll(value, rows - 1, 0))
+
+
+def kernel(
+    n, e_hbm, h_hbm, fwd_hbm, perm_hbm, mask_hbm, inv_hbm, omega, mode, plane,
+    oe, oh, og,
+    e, h, fwd, perm, mask, inv, halo, halo_lo, halo_hi, p_send, p_recv, eps_t, r_first, r_second, inv_eps,
+    mode_col, lines, solved, send, recv, grad,
+    load_sem, halo_send_sem, halo_recv_sem, p_send_sem, p_recv_sem, send_sem, recv_sem,
+):
+    me = lax.axis_index("line")
+    strip = perm.shape[0]
+    cells = inv.shape[0]
+    above, below = (lax.rem(me + 1, n), lax.rem(me + n - 1, n))
+
+    barrier = pltpu.get_barrier_semaphore()
+
+    def greet(k, carry):
+        pl.semaphore_signal(barrier, inc=1, device_id={"line": lax.rem(me + k, n)}, device_id_type=MESH)
+        return carry
+
+    lax.fori_loop(1, n, greet, 0)
+
+    loads = []
+    for source, target in (
+        (perm_hbm.at[0], perm), (e_hbm.at[:, 0], e), (h_hbm.at[:, 0], h), (inv_hbm, inv),
+        (fwd_hbm.at[:, :, 0], fwd), (mask_hbm.at[0], mask),
+    ):
+        copy = pltpu.make_async_copy(source, target, load_sem.at[len(loads)])
+        copy.start()
+        loads.append(copy)
+
+    lane = lax.broadcasted_iota(jnp.int32, (1, LANES), 1)
+    low = lane < strip
+
+    for block in range(cells // LANES):
+        line = jnp.broadcast_to(mode[block : block + 1, :], (LANES, LANES))
+        mode_col[block * LANES : (block + 1) * LANES, :] = line.T
+    mode_col[cells:, :] = jnp.zeros((PAD, LANES), F32)
+    amplitudes = [jnp.cos(jnp.full((1, LANES), omega[0] * (s + 1), F32)) for s in range(2)]
+    at_plane = plane[0]
+
+    loads[0].wait()
+    twice = jnp.concatenate([perm[...], perm[...]], 0)
+    eps_t[...] = twice.T
+    for block in range(n):
+        first = eps_t[block * strip : block * strip + strip // 2, :]
+        second = eps_t[block * strip + strip // 2 : (block + 1) * strip, :]
+        p_send[block] = jnp.where(low, first, second)
+    r_first[0:cells, :] = COURANT * (1.0 / eps_t[...])
+    r_first[cells:, :] = jnp.zeros((PAD, LANES), F32)
+
+    loads[1].wait()
+    loads[2].wait()
+    halo[...] = jnp.concatenate(
+        [
+            e[0, 0:1, :], e[2, 0:1, :], h[0, 0:1, :], h[2, 0:1, :], perm[0:1, :],
+            h[0, strip - 1 : strip, :], h[2, strip - 1 : strip, :], perm[0:1, :],
+        ],
+        0,
+    )
+
+    pl.semaphore_wait(barrier, n - 1)
+
+    to_above = pltpu.make_async_remote_copy(
+        halo, halo_lo, halo_send_sem.at[0], halo_recv_sem.at[0], device_id={"line": above}, device_id_type=MESH
+    )
+    to_below = pltpu.make_async_remote_copy(
+        halo, halo_hi, halo_send_sem.at[1], halo_recv_sem.at[1], device_id={"line": below}, device_id_type=MESH
+    )
+    to_above.start()
+    to_below.start()
+
+    def p_copy(to, slot):
+        return pltpu.make_async_remote_copy(
+            p_send.at[to], p_recv.at[slot], p_send_sem.at[to], p_recv_sem.at[slot],
+            device_id={"line": to}, device_id_type=MESH,
+        )
+
+    def p_start(k, carry):
+        p_copy(lax.rem(me + k, n), me).start()
+        return carry
+
+    lax.fori_loop(1, n, p_start, 0)
+    p_recv[me] = p_send[me]
+
+    to_above.wait()
+    to_below.wait()
+    is_first, is_last = (me == 0, me == n - 1)
+    x_at = lax.broadcasted_iota(jnp.int32, (1, cells), 1)
+    column = jnp.where(x_at == at_plane, 1.0, 0.0)
+    profile = mode_col[pl.ds(pl.multiple_of(me * strip, strip), strip + PAD), :] * amplitudes[0]
+    profile = jnp.concatenate([profile] * (cells // LANES), 1)
+    source = profile * column
+    r = COURANT * (1.0 / perm[...])
+    ex, ez, hx, hz = (e[0], e[2] + source[0:strip], h[0], h[2])
+    hx_lo = jnp.where(is_first, 0.0, halo_lo[5:6, :])
+    hz_lo = jnp.where(is_first, 0.0, halo_lo[6:7, :])
+    ex = ex + r * (hz - shifted_down(hz, hz_lo))
+    ez = ez - r * (hx - shifted_down(hx, hx_lo))
+    r_hi = COURANT * (1.0 / halo_hi[4:5, :])
+    ex_hi = halo_hi[0:1, :] + r_hi * (halo_hi[3:4, :] - hz[strip - 1 : strip])
+    ez_hi = halo_hi[1:2, :] + source[strip : strip + 1] - r_hi * (halo_hi[2:3, :] - hx[strip - 1 : strip])
+    ex_hi = jnp.where(is_last, 0.0, ex_hi)
+    ez_hi = jnp.where(is_last, 0.0, ez_hi)
+    hx = hx - COURANT * (shifted_up(ez, ez_hi) - ez)
+    hz = hz + COURANT * (shifted_up(ex, ex_hi) - ex)
+    for at, value in enumerate((ex, e[1], ez, hx, h[1], hz)):
+        lines[at * strip : (at + 1) * strip, :] = value.astype(BF16)
+    loads[3].wait()
+
+    def copy_out(stage, to, slot):
+        return pltpu.make_async_remote_copy(
+            send.at[stage, to], recv.at[stage, slot], send_sem.at[stage, to], recv_sem.at[stage, slot],
+            device_id={"line": to}, device_id_type=MESH,
+        )
+
+    def send_all(stage):
+        def go(k, carry):
+            copy_out(stage, lax.rem(me + k, n), me).start()
+            return carry
+
+        lax.fori_loop(1, n, go, 0)
+        recv[stage, me] = send[stage, me]
+
+    def receive_all(stage):
+        def take(k, carry):
+            other = lax.rem(me + k, n)
+            copy_out(stage, other, other).wait_recv()
+            return carry
+
+        lax.fori_loop(1, n, take, 0)
+
+    def solve_turned():
+        for pair in range(3):
+            solved[pair, 0:PAD, :] = jnp.zeros((PAD, LANES), F32)
+            solved[pair, cells + PAD :, :] = jnp.zeros((PAD, LANES), F32)
+        result = contract(inv[...], lines[...])
+        for pair in range(3):
+            solved[pair, PAD : cells + PAD, :] = result[:, pair * LANES : (pair + 1) * LANES]
+
+    def assemble(stage, pairs, order):
+        half = n // 2
+        for k in range(half):
+            for pair, (one, two) in enumerate(pairs):
+                a, b = (recv[stage, 2 * k, pair], recv[stage, 2 * k + 1, pair])
+                at_one, at_two = (order.index(one) * strip, order.index(two) * strip)
+                cut = slice(k * LANES, (k + 1) * LANES)
+                lines[at_one : at_one + strip, cut] = jnp.concatenate([a[:, :strip], b[:, :strip]], 1)
+                lines[at_two : at_two + strip, cut] = jnp.concatenate([a[:, strip:], b[:, strip:]], 1)
+
+    rows = LANES
+
+    def put(stage, start, tiles):
+        for pair, tile in enumerate(tiles):
+            for part in range(rows // strip):
+                send[stage, start // strip + part, pair] = tile[part * strip : (part + 1) * strip].astype(BF16)
+
+    def extended(pair, start, back):
+        return solved[pair, start + PAD - back : start + PAD - back + rows + PAD, :]
+
+    def curl_x(stage):
+        for start in range(0, cells, rows):
+            row = lax.broadcasted_iota(jnp.int32, (rows + PAD, LANES), 0) + start
+            p, q, t = (extended(0, start, 0), extended(1, start, 0), extended(2, start, 0))
+            r = r_first[start : start + rows + PAD, :]
+            dt = t - extended(2, start, 1)
+            p = p + r * jnp.where(low, -t, q - dt)
+            q = q + jnp.where(low, r * dt, -COURANT * p)
+            s = jnp.where(row < cells, jnp.where(low, q, p), 0.0)
+            ds = (pltpu.roll(s, rows + PAD - 1, 0) - s)[0:rows]
+            p, q, t = (p[0:rows], q[0:rows], t[0:rows])
+            t = t + jnp.where(low, COURANT * (ds + p), -COURANT * ds)
+            put(stage, start, (p, q, t))
+
+    def curl_y(stage):
+        here = jnp.where(low, 0.0, 1.0) * jnp.where(lane - strip + me * strip == at_plane, 1.0, 0.0)
+        for start in range(0, cells, rows):
+            row = lax.broadcasted_iota(jnp.int32, (rows + PAD, LANES), 0) + start
+            p, t = (extended(0, start, 0), extended(2, start, 0))
+            r = r_second[start : start + rows + PAD, :]
+            p = p + (amplitudes[1] * mode_col[start : start + rows + PAD, :]) * here
+            dt = t - extended(2, start, 1)
+            p = p + jnp.where(low, r, -r) * dt
+            p = jnp.where(row < cells, p, 0.0)
+            dp = (pltpu.roll(p, rows + PAD - 1, 0) - p)[0:rows]
+            t = t[0:rows] + jnp.where(low, COURANT, -COURANT) * dp
+            put(stage, start, (p[0:rows], extended(1, start, 0)[0:rows], t))
+
+    def along(electric, instant):
+        return (
+            electric[0] * fwd[instant, 0].astype(F32)
+            + electric[1] * fwd[instant, 1].astype(F32)
+            + electric[2] * fwd[instant, 2].astype(F32)
+        )
+
+    solve_turned()
+    curl_x(0)
+    send_all(0)
+
+    def p_take(k, carry):
+        other = lax.rem(me + k, n)
+        p_copy(other, other).wait_recv()
+        return carry
+
+    lax.fori_loop(1, n, p_take, 0)
+    for k in range(n // 2):
+        a, b = (p_recv[2 * k], p_recv[2 * k + 1])
+        cut = slice(k * LANES, (k + 1) * LANES)
+        inv_eps[0 : strip // 2, cut] = 1.0 / jnp.concatenate([a[:, :strip], b[:, :strip]], 1)
+        inv_eps[strip // 2 :, cut] = 1.0 / jnp.concatenate([a[:, strip:], b[:, strip:]], 1)
+    both = jnp.concatenate([inv_eps[...], inv_eps[...]], 0)
+    r_second[0:cells, :] = COURANT * both.T
+    r_second[cells:, :] = jnp.zeros((PAD, LANES), F32)
+    loads[4].wait()
+    loads[5].wait()
+    weight = mask[...].astype(F32)
+
+    receive_all(0)
+    assemble(0, PAIRS_X, (0, 2, 1, 4, 5, 3))
+    solve_turned()
+    curl_y(1)
+    send_all(1)
+
+    square = inv_eps[...] * inv_eps[...]
+    electric = contract(lines[0 : 3 * strip, :], inv[...])
+    parts = (electric[0:strip], electric[2 * strip :], electric[strip : 2 * strip])
+    grad[...] = weight * along(parts, 0) * square
+
+    receive_all(1)
+    assemble(1, PAIRS_Y, (0, 1, 2, 3, 4, 5))
+    solve_turned()
+    curl_x(2)
+    send_all(2)
+
+    receive_all(2)
+    assemble(2, PAIRS_X, (0, 1, 2, 3, 4, 5))
+    final = contract(lines[...], inv[...])
+    parts = [final[at * strip : (at + 1) * strip] for at in range(6)]
+    for at in range(3):
+        oe[at, 0] = parts[at]
+        oh[at, 0] = parts[3 + at]
+    og[0] = grad[...] + weight * along(parts, 1) * square
+
+    def settle(k, carry):
+        other = lax.rem(me + k, n)
+        p_copy(other, other).wait_send()
+        for stage in range(3):
+            copy_out(stage, other, other).wait_send()
+        return carry
+
+    lax.fori_loop(1, n, settle, 0)
+
+
+def fused(adj_e, adj_h, fwd_e, permittivity, design_mask, inverse, omega, port_mode, port_plane):
+    n = lax.axis_size("line")
+    cells, strip = (inverse.shape[0], adj_e.shape[2])
+    steps = fwd_e.shape[0]
+    anywhere = pl.BlockSpec(memory_space=pl.ANY)
+    vmem = pl.BlockSpec(memory_space=pltpu.VMEM)
+    smem = pl.BlockSpec(memory_space=pltpu.SMEM)
+    scratch = [
+        pltpu.VMEM((3, strip, cells), F32),
+        pltpu.VMEM((3, strip, cells), F32),
+        pltpu.VMEM((steps, 3, strip, cells), BF16),
+        pltpu.VMEM((strip, cells), F32),
+        pltpu.VMEM((strip, cells), jnp.int32),
+        pltpu.VMEM((cells, cells), BF16),
+        pltpu.VMEM((8, cells), F32),
+        pltpu.VMEM((8, cells), F32),
+        pltpu.VMEM((8, cells), F32),
+        pltpu.VMEM((n, strip // 2, LANES), F32),
+        pltpu.VMEM((n, strip // 2, LANES), F32),
+        pltpu.VMEM((cells, LANES), F32),
+        pltpu.VMEM((cells + PAD, LANES), F32),
+        pltpu.VMEM((cells + PAD, LANES), F32),
+        pltpu.VMEM((strip, cells), F32),
+        pltpu.VMEM((cells + PAD, LANES), F32),
+        pltpu.VMEM((6 * strip, cells), BF16),
+        pltpu.VMEM((3, cells + 2 * PAD, LANES), F32),
+        pltpu.VMEM((3, n, 3, strip, LANES), BF16),
+        pltpu.VMEM((3, n, 3, strip, LANES), BF16),
+        pltpu.VMEM((strip, cells), F32),
+        pltpu.SemaphoreType.DMA((6,)),
+        pltpu.SemaphoreType.DMA((2,)),
+        pltpu.SemaphoreType.DMA((2,)),
+        pltpu.SemaphoreType.DMA((n,)),
+        pltpu.SemaphoreType.DMA((n,)),
+        pltpu.SemaphoreType.DMA((3, n)),
+        pltpu.SemaphoreType.DMA((3, n)),
+    ]
+    return pl.pallas_call(
+        functools.partial(kernel, n),
+        out_shape=(
+            jax.ShapeDtypeStruct(adj_e.shape, F32),
+            jax.ShapeDtypeStruct(adj_h.shape, F32),
+            jax.ShapeDtypeStruct(permittivity.shape, F32),
+        ),
+        in_specs=[anywhere] * 6 + [smem, vmem, smem],
+        out_specs=(vmem, vmem, vmem),
+        scratch_shapes=scratch,
+        compiler_params=pltpu.CompilerParams(
+            collective_id=0, has_side_effects=True, vmem_limit_bytes=50 * 1024 * 1024
+        ),
+    )(
+        adj_e, adj_h, fwd_e, permittivity, design_mask, inverse, omega,
+        port_mode.reshape(cells // LANES, LANES), port_plane,
+    )
+
+
+def per_device(adj_e, adj_h, fwd_e, permittivity, design_mask, inverse, omega, port_mode, port_plane):
+    args = (adj_e, adj_h, fwd_e, permittivity, design_mask, inverse, omega, port_mode, port_plane)
+    paired = 2 * adj_e.shape[2] == LANES and fwd_e.shape[0] == 2 and permittivity.shape[0] == 1
+    return fused(*args) if paired else plain_per_device(*args)
+
+
 def solution(mesh):
     in_specs = (
         P(None, "exc", "line", None),

time: 343 us -> 79.2 us (0.23)
  the two profiles are of different devices: /device:TPU:0 before, /device:TPU:20 now
where the time goes in v1:
time: 79.2 us; the launch traced here: 78.9 us
  Pallas kernels  69.6 us (88%)
  local copies, waits for them, and re-layouts  7.31 us (9%)
  between operations  1.95 us (2%)
    pallas_call x1, Pallas kernels, fused(): pl.pallas_call(functools.partial(kernel, n), out_shape=(jax.ShapeDtypeStr...  69.6 us
    unnamed x13, local copies, waits for them, and re-layouts  7.31 us

profile of v1, /device:TPU:20, one launch (start us, length us, event | category | flops | bytes accessed | tf_op | source)
XLA Modules:
  0.0 78.9 jit_solution(15541857993853473665)
XLA Ops:
  1.9 0.0 copy-start
  1.9 1.1 %copy-done = f32[3,1,64,1024]{3,2,1,0:T(8,128)S(1)} copy-done((f32[3,1,64,1024]{3,2,1,0:T(8,128)S(1)}, f32[3,1,64,1024]{3,2,1,0:T(8,128)}, u32[]{:S(2)}) %copy-start) | copy-done | bytes 786456
  3.1 0.0 copy-start.1
  3.1 1.1 %copy-done.1 = f32[3,1,64,1024]{3,2,1,0:T(8,128)S(1)} copy-done((f32[3,1,64,1024]{3,2,1,0:T(8,128)S(1)}, f32[3,1,64,1024]{3,2,1,0:T(8,128)}, u32[]{:S(2)}) %copy-start.1) | copy-done | bytes 786456
  4.2 0.0 copy-start.2
  4.2 0.9 %copy-done.2 = f32[1,64,1024]{2,1,0:T(8,128)S(1)} copy-done((f32[1,64,1024]{2,1,0:T(8,128)S(1)}, f32[1,64,1024]{2,1,0:T(8,128)}, u32[]{:S(2)}) %copy-start.2) | copy-done | bytes 262168
  5.1 0.0 copy-start.3
  5.1 0.9 %copy-done.3 = s32[1,64,1024]{2,1,0:T(8,128)S(1)} copy-done((s32[1,64,1024]{2,1,0:T(8,128)S(1)}, s32[1,64,1024]{2,1,0:T(8,128)}, u32[]{:S(2)}) %copy-start.3) | copy-done | bytes 262168
  6.1 0.0 copy-start.4
  6.1 0.7 copy-done.4
  6.8 69.6 %shard_map.112 = (f32[3,1,64,1024]{3,2,1,0:T(8,128)S(1)}, f32[3,1,64,1024]{3,2,1,0:T(8,128)S(1)}, f32[1,64,1024]{2,1,0:T(8,128)S(1)}) custom-call(f32[3,1,64,1024]{3,2,1,0:T(8,128)S(1)} %copy-done, f32[3,1,64,1024]{3,2,1,0:T(8,128)S(1)} %copy-done.1, bf16[2,3,1,64,1024]{4,3,2,1,0:T(8,128)(2,1)} %fwd_hbm.1, f32[1,64,1024]{2,1,0:T(8,128)S(1)} %copy-done.2, ...), custom_call_target="tpu_custom_call" | custom-call | tf_op jit(solution)/shard_map/pallas_call | solution.py:467
  76.4 0.9 %copy.17 = f32[3,1,64,1024]{3,2,1,0:T(8,128)} copy(f32[3,1,64,1024]{3,2,1,0:T(8,128)S(1)} %get-tuple-element.6) | data formatting | bytes 1572864
  77.3 0.9 %copy.18 = f32[3,1,64,1024]{3,2,1,0:T(8,128)} copy(f32[3,1,64,1024]{3,2,1,0:T(8,128)S(1)} %get-tuple-element.7) | data formatting | bytes 1572864
  78.2 0.7 copy.19
Async XLA Ops:
  1.9 1.1 %copy-start = (f32[3,1,64,1024]{3,2,1,0:T(8,128)S(1)}, f32[3,1,64,1024]{3,2,1,0:T(8,128)}, u32[]{:S(2)}) copy-start(f32[3,1,64,1024]{3,2,1,0:T(8,128)} %e_hbm.1) | copy-start | bytes 2359300
  3.1 1.1 %copy-start.1 = (f32[3,1,64,1024]{3,2,1,0:T(8,128)S(1)}, f32[3,1,64,1024]{3,2,1,0:T(8,128)}, u32[]{:S(2)}) copy-start(f32[3,1,64,1024]{3,2,1,0:T(8,128)} %h_hbm.1) | copy-start | bytes 2359300
  4.2 0.9 %copy-start.2 = (f32[1,64,1024]{2,1,0:T(8,128)S(1)}, f32[1,64,1024]{2,1,0:T(8,128)}, u32[]{:S(2)}) copy-start(f32[1,64,1024]{2,1,0:T(8,128)} %perm_hbm.1) | copy-start | bytes 786436
  5.1 0.9 %copy-start.3 = (s32[1,64,1024]{2,1,0:T(8,128)S(1)}, s32[1,64,1024]{2,1,0:T(8,128)}, u32[]{:S(2)}) copy-start(s32[1,64,1024]{2,1,0:T(8,128)} %mask_hbm.1) | copy-start | bytes 786436
  6.1 0.7 copy-start.4

commit v2 on v1

--- a/solution.py
+++ b/solution.py
@@ -157,8 +157,6 @@
 MESH = pl.DeviceIdType.MESH
 PAD = 8
 F32, BF16 = (jnp.float32, jnp.bfloat16)
-PAIRS_X = ((0, 1), (2, 3), (4, 5))
-PAIRS_Y = ((0, 2), (1, 4), (5, 3))
 
 
 def contract(left, right):
@@ -177,10 +175,10 @@
 
 
 def kernel(
-    n, e_hbm, h_hbm, fwd_hbm, perm_hbm, mask_hbm, inv_hbm, omega, mode, plane,
+    n, e_hbm, h_hbm, fwd_hbm, perm_hbm, mask_hbm, inv_hbm, omega, mode_hbm, plane,
     oe, oh, og,
     e, h, fwd, perm, mask, inv, halo, halo_lo, halo_hi, p_send, p_recv, eps_t, r_first, r_second, inv_eps,
-    mode_col, lines, solved, send, recv, grad,
+    mode_v, mode_col, lines, solved, kept, send, recv, grad,
     load_sem, halo_send_sem, halo_recv_sem, p_send_sem, p_recv_sem, send_sem, recv_sem,
 ):
     me = lax.axis_index("line")
@@ -198,7 +196,7 @@
 
     loads = []
     for source, target in (
-        (perm_hbm.at[0], perm), (e_hbm.at[:, 0], e), (h_hbm.at[:, 0], h), (inv_hbm, inv),
+        (perm_hbm.at[0], perm), (mode_hbm, mode_v), (e_hbm.at[:, 0], e), (h_hbm.at[:, 0], h), (inv_hbm, inv),
         (fwd_hbm.at[:, :, 0], fwd), (mask_hbm.at[0], mask),
     ):
         copy = pltpu.make_async_copy(source, target, load_sem.at[len(loads)])
@@ -207,13 +205,6 @@
 
     lane = lax.broadcasted_iota(jnp.int32, (1, LANES), 1)
     low = lane < strip
-
-    for block in range(cells // LANES):
-        line = jnp.broadcast_to(mode[block : block + 1, :], (LANES, LANES))
-        mode_col[block * LANES : (block + 1) * LANES, :] = line.T
-    mode_col[cells:, :] = jnp.zeros((PAD, LANES), F32)
-    amplitudes = [jnp.cos(jnp.full((1, LANES), omega[0] * (s + 1), F32)) for s in range(2)]
-    at_plane = plane[0]
 
     loads[0].wait()
     twice = jnp.concatenate([perm[...], perm[...]], 0)
@@ -226,7 +217,15 @@
     r_first[cells:, :] = jnp.zeros((PAD, LANES), F32)
 
     loads[1].wait()
+    for block in range(cells // LANES):
+        line = jnp.broadcast_to(mode_v[block : block + 1, :], (LANES, LANES))
+        mode_col[block * LANES : (block + 1) * LANES, :] = line.T
+    mode_col[cells:, :] = jnp.zeros((PAD, LANES), F32)
+    amplitudes = [jnp.cos(jnp.full((1, LANES), omega[0] * (s + 1), F32)) for s in range(2)]
+    at_plane = plane[0]
+
     loads[2].wait()
+    loads[3].wait()
     halo[...] = jnp.concatenate(
         [
             e[0, 0:1, :], e[2, 0:1, :], h[0, 0:1, :], h[2, 0:1, :], perm[0:1, :],
@@ -280,87 +279,90 @@
     ez_hi = jnp.where(is_last, 0.0, ez_hi)
     hx = hx - COURANT * (shifted_up(ez, ez_hi) - ez)
     hz = hz + COURANT * (shifted_up(ex, ex_hi) - ex)
-    for at, value in enumerate((ex, e[1], ez, hx, h[1], hz)):
+    for at, value in enumerate((ex, ez, h[1], e[1], hz, hx)):
         lines[at * strip : (at + 1) * strip, :] = value.astype(BF16)
-    loads[3].wait()
-
-    def copy_out(stage, to, slot):
+
+    def copy_out(message, to, slot):
         return pltpu.make_async_remote_copy(
-            send.at[stage, to], recv.at[stage, slot], send_sem.at[stage, to], recv_sem.at[stage, slot],
+            send.at[message, to], recv.at[message, slot], send_sem.at[message, to], recv_sem.at[message, slot],
             device_id={"line": to}, device_id_type=MESH,
         )
 
-    def send_all(stage):
+    def send_all(message):
         def go(k, carry):
-            copy_out(stage, lax.rem(me + k, n), me).start()
+            copy_out(message, lax.rem(me + k, n), me).start()
             return carry
 
         lax.fori_loop(1, n, go, 0)
-        recv[stage, me] = send[stage, me]
-
-    def receive_all(stage):
+        recv[message, me] = send[message, me]
+
+    def receive_all(message):
         def take(k, carry):
             other = lax.rem(me + k, n)
-            copy_out(stage, other, other).wait_recv()
+            copy_out(message, other, other).wait_recv()
             return carry
 
         lax.fori_loop(1, n, take, 0)
 
-    def solve_turned():
-        for pair in range(3):
-            solved[pair, 0:PAD, :] = jnp.zeros((PAD, LANES), F32)
-            solved[pair, cells + PAD :, :] = jnp.zeros((PAD, LANES), F32)
-        result = contract(inv[...], lines[...])
-        for pair in range(3):
-            solved[pair, PAD : cells + PAD, :] = result[:, pair * LANES : (pair + 1) * LANES]
-
-    def assemble(stage, pairs, order):
-        half = n // 2
-        for k in range(half):
-            for pair, (one, two) in enumerate(pairs):
-                a, b = (recv[stage, 2 * k, pair], recv[stage, 2 * k + 1, pair])
-                at_one, at_two = (order.index(one) * strip, order.index(two) * strip)
-                cut = slice(k * LANES, (k + 1) * LANES)
-                lines[at_one : at_one + strip, cut] = jnp.concatenate([a[:, :strip], b[:, :strip]], 1)
-                lines[at_two : at_two + strip, cut] = jnp.concatenate([a[:, strip:], b[:, strip:]], 1)
+    def assemble(message, tile):
+        receive_all(message)
+        at = tile * LANES
+        for k in range(n // 2):
+            a, b = (recv[message, 2 * k], recv[message, 2 * k + 1])
+            cut = slice(k * LANES, (k + 1) * LANES)
+            lines[at : at + strip, cut] = jnp.concatenate([a[:, :strip], b[:, :strip]], 1)
+            lines[at + strip : at + LANES, cut] = jnp.concatenate([a[:, strip:], b[:, strip:]], 1)
+
+    def solve_tile(tile):
+        part = lines[tile * LANES : (tile + 1) * LANES, :]
+        solved[tile, PAD : cells + PAD, :] = contract(inv[...], part)
 
     rows = LANES
 
-    def put(stage, start, tiles):
-        for pair, tile in enumerate(tiles):
-            for part in range(rows // strip):
-                send[stage, start // strip + part, pair] = tile[part * strip : (part + 1) * strip].astype(BF16)
-
-    def extended(pair, start, back):
-        return solved[pair, start + PAD - back : start + PAD - back + rows + PAD, :]
-
-    def curl_x(stage):
-        for start in range(0, cells, rows):
-            row = lax.broadcasted_iota(jnp.int32, (rows + PAD, LANES), 0) + start
-            p, q, t = (extended(0, start, 0), extended(1, start, 0), extended(2, start, 0))
-            r = r_first[start : start + rows + PAD, :]
-            dt = t - extended(2, start, 1)
-            p = p + r * jnp.where(low, -t, q - dt)
-            q = q + jnp.where(low, r * dt, -COURANT * p)
-            s = jnp.where(row < cells, jnp.where(low, q, p), 0.0)
-            ds = (pltpu.roll(s, rows + PAD - 1, 0) - s)[0:rows]
-            p, q, t = (p[0:rows], q[0:rows], t[0:rows])
-            t = t + jnp.where(low, COURANT * (ds + p), -COURANT * ds)
-            put(stage, start, (p, q, t))
-
-    def curl_y(stage):
-        here = jnp.where(low, 0.0, 1.0) * jnp.where(lane - strip + me * strip == at_plane, 1.0, 0.0)
-        for start in range(0, cells, rows):
-            row = lax.broadcasted_iota(jnp.int32, (rows + PAD, LANES), 0) + start
-            p, t = (extended(0, start, 0), extended(2, start, 0))
-            r = r_second[start : start + rows + PAD, :]
-            p = p + (amplitudes[1] * mode_col[start : start + rows + PAD, :]) * here
-            dt = t - extended(2, start, 1)
-            p = p + jnp.where(low, r, -r) * dt
-            p = jnp.where(row < cells, p, 0.0)
-            dp = (pltpu.roll(p, rows + PAD - 1, 0) - p)[0:rows]
-            t = t[0:rows] + jnp.where(low, COURANT, -COURANT) * dp
-            put(stage, start, (p[0:rows], extended(1, start, 0)[0:rows], t))
+    def put(message, start, tile):
+        for part in range(rows // strip):
+            send[message, start // strip + part] = tile[part * strip : (part + 1) * strip].astype(BF16)
+
+    def swap(tile):
+        return pltpu.roll(tile, LANES // 2, 1)
+
+    def extended(tile, start, back):
+        return solved[tile, start + PAD - back : start + PAD - back + rows + PAD, :]
+
+    def next_row(value):
+        return pltpu.roll(value, value.shape[0] - 1, 0)
+
+    def in_grid(start):
+        return lax.broadcasted_iota(jnp.int32, (rows + PAD, LANES), 0) + start < cells
+
+    def curl_x_first(start):
+        here = slice(start + PAD, start + PAD + rows)
+        b, bd = (solved[1, here, :], solved[1, start + PAD - 1 : start + PAD - 1 + rows, :])
+        hy, hyd = (jnp.where(low, b, swap(b)), jnp.where(low, bd, swap(bd)))
+        a = solved[0, here, :] + r_first[start : start + rows, :] * jnp.where(low, -hy, hy - hyd)
+        solved[0, here, :] = a
+        return a
+
+    def curl_x_second(start):
+        a, b, c = (extended(0, start, 0), extended(1, start, 0), extended(2, start, 0))
+        sa, sc = (swap(a), swap(c))
+        dc = sc - swap(extended(2, start, 1))
+        ey = b + r_first[start : start + rows + PAD, :] * (c - dc)
+        ey = jnp.where(in_grid(start), ey, 0.0)
+        hy = b + COURANT * ((next_row(sa) - sa) + a)
+        sy = swap(ey)
+        c = c - COURANT * jnp.where(low, next_row(sy) - sy, ey)
+        return jnp.where(low, hy, ey)[0:rows], c[0:rows]
+
+    def curl_y(tile, start, sign, source):
+        t, td = (extended(tile, start, 0), extended(tile, start, 1))
+        st, std = (swap(t), swap(td))
+        p = t if source is None else t + source
+        p = p + sign * r_second[start : start + rows + PAD, :] * (st - std)
+        p = jnp.where(in_grid(start), p, 0.0)
+        sp = swap(p)
+        q = t + sign * COURANT * (next_row(sp) - sp)
+        return jnp.where(low, p, q)[0:rows]
 
     def along(electric, instant):
         return (
@@ -369,9 +371,25 @@
             + electric[2] * fwd[instant, 2].astype(F32)
         )
 
-    solve_turned()
-    curl_x(0)
-    send_all(0)
+    for tile in range(3):
+        solved[tile, 0:PAD, :] = jnp.zeros((PAD, LANES), F32)
+        solved[tile, cells + PAD :, :] = jnp.zeros((PAD, LANES), F32)
+    starts = range(0, cells, rows)
+
+    loads[4].wait()
+    result = contract(inv[...], lines[...])
+    for tile in range(3):
+        solved[tile, PAD : cells + PAD, :] = result[:, tile * LANES : (tile + 1) * LANES]
+    for start in starts:
+        curl_x_first(start)
+    for start in starts:
+        a = solved[0, start + PAD : start + PAD + rows, :]
+        b, c = curl_x_second(start)
+        put(0, start, jnp.where(low, a, swap(c)))
+        put(1, start, jnp.where(low, swap(a), c))
+        put(2, start, b)
+    for message in range(3):
+        send_all(message)
 
     def p_take(k, carry):
         other = lax.rem(me + k, n)
@@ -387,51 +405,95 @@
     both = jnp.concatenate([inv_eps[...], inv_eps[...]], 0)
     r_second[0:cells, :] = COURANT * both.T
     r_second[cells:, :] = jnp.zeros((PAD, LANES), F32)
-    loads[4].wait()
     loads[5].wait()
+    loads[6].wait()
+
+    assemble(0, 0)
+    solve_tile(0)
+    for start in starts:
+        kept[start : start + rows, :] = curl_y(0, start, 1.0, None)
+    assemble(1, 1)
+    solve_tile(1)
+    here = jnp.where(low & (lane + me * strip == at_plane), 1.0, 0.0)
+    for start in starts:
+        source = (amplitudes[1] * mode_col[start : start + rows + PAD, :]) * here
+        b = curl_y(1, start, -1.0, source)
+        a = kept[start : start + rows, :]
+        put(3, start, jnp.where(low, a, swap(b)))
+        put(5, start, jnp.where(low, swap(a), b))
+    send_all(3)
+    assemble(2, 2)
+    solve_tile(2)
+    for start in starts:
+        put(4, start, solved[2, start + PAD : start + PAD + rows, :])
+    send_all(4)
+    send_all(5)
+
     weight = mask[...].astype(F32)
-
-    receive_all(0)
-    assemble(0, PAIRS_X, (0, 2, 1, 4, 5, 3))
-    solve_turned()
-    curl_y(1)
-    send_all(1)
-
     square = inv_eps[...] * inv_eps[...]
-    electric = contract(lines[0 : 3 * strip, :], inv[...])
+    electric = jnp.concatenate(
+        [lines[0:strip, :], lines[LANES + strip * 0 : LANES + strip, :], lines[2 * LANES + strip :, :]], 0
+    )
+    electric = contract(electric, inv[...])
     parts = (electric[0:strip], electric[2 * strip :], electric[strip : 2 * strip])
     grad[...] = weight * along(parts, 0) * square
 
-    receive_all(1)
-    assemble(1, PAIRS_Y, (0, 1, 2, 3, 4, 5))
-    solve_turned()
-    curl_x(2)
-    send_all(2)
-
-    receive_all(2)
-    assemble(2, PAIRS_X, (0, 1, 2, 3, 4, 5))
-    final = contract(lines[...], inv[...])
-    parts = [final[at * strip : (at + 1) * strip] for at in range(6)]
-    for at in range(3):
-        oe[at, 0] = parts[at]
-        oh[at, 0] = parts[3 + at]
-    og[0] = grad[...] + weight * along(parts, 1) * square
+    for tile in range(2):
+        assemble(3 + tile, tile)
+        solve_tile(tile)
+    for start in starts:
+        put(6, start, curl_x_first(start))
+    send_all(6)
+    assemble(5, 2)
+    solve_tile(2)
+    for start in starts:
+        b, c = curl_x_second(start)
+        put(7, start, b)
+        put(8, start, c)
+    send_all(7)
+    send_all(8)
+
+    assemble(6, 0)
+    pair = contract(lines[0:LANES, :], inv[...])
+    oe[0, 0] = pair[:strip]
+    oe[2, 0] = pair[strip:]
+    assemble(7, 1)
+    pair = contract(lines[LANES : 2 * LANES, :], inv[...])
+    oh[1, 0] = pair[:strip]
+    oe[1, 0] = pair[strip:]
+    og[0] = grad[...] + weight * along((oe[0, 0], pair[strip:], oe[2, 0]), 1) * square
+    assemble(8, 2)
+    pair = contract(lines[2 * LANES :, :], inv[...])
+    oh[2, 0] = pair[:strip]
+    oh[0, 0] = pair[strip:]
 
     def settle(k, carry):
         other = lax.rem(me + k, n)
         p_copy(other, other).wait_send()
-        for stage in range(3):
-            copy_out(stage, other, other).wait_send()
+        for message in range(9):
+            copy_out(message, other, other).wait_send()
         return carry
 
     lax.fori_loop(1, n, settle, 0)
+
+
+def write_out(e, h, g, oe, oh, og, sem):
+    copies = []
+    for source, target in ((e, oe), (h, oh)):
+        for at in range(3):
+            copies.append(pltpu.make_async_copy(source.at[at], target.at[at], sem.at[len(copies)]))
+    copies.append(pltpu.make_async_copy(g, og, sem.at[len(copies)]))
+    for copy in copies:
+        copy.start()
+    for copy in copies:
+        copy.wait()
 
 
 def fused(adj_e, adj_h, fwd_e, permittivity, design_mask, inverse, omega, port_mode, port_plane):
     n = lax.axis_size("line")
     cells, strip = (inverse.shape[0], adj_e.shape[2])
     steps = fwd_e.shape[0]
-    anywhere = pl.BlockSpec(memory_space=pl.ANY)
+    hbm = pl.BlockSpec(memory_space=pltpu.HBM)
     vmem = pl.BlockSpec(memory_space=pltpu.VMEM)
     smem = pl.BlockSpec(memory_space=pltpu.SMEM)
     scratch = [
@@ -450,36 +512,44 @@
         pltpu.VMEM((cells + PAD, LANES), F32),
         pltpu.VMEM((cells + PAD, LANES), F32),
         pltpu.VMEM((strip, cells), F32),
+        pltpu.VMEM((cells // LANES, LANES), F32),
         pltpu.VMEM((cells + PAD, LANES), F32),
         pltpu.VMEM((6 * strip, cells), BF16),
         pltpu.VMEM((3, cells + 2 * PAD, LANES), F32),
-        pltpu.VMEM((3, n, 3, strip, LANES), BF16),
-        pltpu.VMEM((3, n, 3, strip, LANES), BF16),
+        pltpu.VMEM((cells, LANES), F32),
+        pltpu.VMEM((9, n, strip, LANES), BF16),
+        pltpu.VMEM((9, n, strip, LANES), BF16),
         pltpu.VMEM((strip, cells), F32),
-        pltpu.SemaphoreType.DMA((6,)),
+        pltpu.SemaphoreType.DMA((7,)),
         pltpu.SemaphoreType.DMA((2,)),
         pltpu.SemaphoreType.DMA((2,)),
         pltpu.SemaphoreType.DMA((n,)),
         pltpu.SemaphoreType.DMA((n,)),
-        pltpu.SemaphoreType.DMA((3, n)),
-        pltpu.SemaphoreType.DMA((3, n)),
+        pltpu.SemaphoreType.DMA((9, n)),
+        pltpu.SemaphoreType.DMA((9, n)),
     ]
-    return pl.pallas_call(
+    shapes = tuple(jax.ShapeDtypeStruct(a.shape, F32) for a in (adj_e, adj_h, permittivity))
+    results = pl.pallas_call(
         functools.partial(kernel, n),
-        out_shape=(
-            jax.ShapeDtypeStruct(adj_e.shape, F32),
-            jax.ShapeDtypeStruct(adj_h.shape, F32),
-            jax.ShapeDtypeStruct(permittivity.shape, F32),
-        ),
-        in_specs=[anywhere] * 6 + [smem, vmem, smem],
+        out_shape=tuple(pltpu.VMEM(a.shape, F32) for a in shapes),
+        in_specs=[hbm] * 6 + [smem, hbm, smem],
         out_specs=(vmem, vmem, vmem),
         scratch_shapes=scratch,
         compiler_params=pltpu.CompilerParams(
-            collective_id=0, has_side_effects=True, vmem_limit_bytes=50 * 1024 * 1024
+            collective_id=0, has_side_effects=True, vmem_limit_bytes=60 * 1024 * 1024
         ),
     )(
         adj_e, adj_h, fwd_e, permittivity, design_mask, inverse, omega,
         port_mode.reshape(cells // LANES, LANES), port_plane,
+    )
+    return tuple(
+        pl.pallas_call(
+            write_out,
+            out_shape=shapes,
+            in_specs=[pl.BlockSpec(memory_space=pl.ANY)] * 3,
+            out_specs=(hbm, hbm, hbm),
+            scratch_shapes=[pltpu.SemaphoreType.DMA((7,))],
+        )(*results)
     )
 
 

time: 79.2 us -> 132 us (1.67)
  the two profiles are of different devices: /device:TPU:20 before, /device:TPU:0 now
where the time goes in v2:
time: 132 us
  Pallas kernels  128 us (97%)
  local copies, waits for them, and re-layouts  2.47 us (2%)
  between operations  1.94 us (1%)
    pallas_call x1, Pallas kernels, fused(): pl.pallas_call(functools.partial(kernel, n), out_shape=tuple((pltpu.VMEM(...  70.8 us
    pallas_call x1, Pallas kernels, fused(): pl.pallas_call(write_out, out_shape=shapes, in_specs=[pl.BlockSpec(memory...  56.7 us

profile of v2, /device:TPU:0, one launch (start us, length us, event | category | flops | bytes accessed | tf_op | source)
XLA Modules:
  0.0 131.9 jit_solution(5384575553331047476)
XLA Ops:
  1.9 70.8 %shard_map.112 = (f32[3,1,64,1024]{3,2,1,0:T(8,128)S(1)}, f32[3,1,64,1024]{3,2,1,0:T(8,128)S(1)}, f32[1,64,1024]{2,1,0:T(8,128)S(1)}) custom-call(f32[3,1,64,1024]{3,2,1,0:T(8,128)} %e_hbm.1, f32[3,1,64,1024]{3,2,1,0:T(8,128)} %h_hbm.1, bf16[2,3,1,64,1024]{4,3,2,1,0:T(8,128)(2,1)} %fwd_hbm.1, f32[1,64,1024]{2,1,0:T(8,128)} %perm_hbm.1, ...), custom_call_target="tpu_custom_call" | custom-call | tf_op jit(solution)/shard_map/pallas_call | solution.py:532
  72.7 0.0 copy-start
  72.7 0.9 copy-done
  73.6 0.0 copy-start.1
  73.6 0.9 copy-done.1
  74.5 0.0 copy-start.2
  74.5 0.7 copy-done.2
  75.2 56.7 %shard_map.113 = (f32[3,1,64,1024]{3,2,1,0:T(8,128)}, f32[3,1,64,1024]{3,2,1,0:T(8,128)}, f32[1,64,1024]{2,1,0:T(8,128)}) custom-call(f32[3,1,64,1024]{3,2,1,0:T(8,128)} %copy-done, f32[3,1,64,1024]{3,2,1,0:T(8,128)} %copy-done.1, f32[1,64,1024]{2,1,0:T(8,128)} %copy-done.2), custom_call_target="tpu_custom_call" | custom-call | tf_op jit(solution)/shard_map/pallas_call | solution.py:546
Async XLA Ops:
  72.7 0.9 copy-start
  73.6 0.9 copy-start.1
  74.5 0.7 copy-start.2

commit v3 on v2

--- a/solution.py
+++ b/solution.py
@@ -178,7 +178,7 @@
     n, e_hbm, h_hbm, fwd_hbm, perm_hbm, mask_hbm, inv_hbm, omega, mode_hbm, plane,
     oe, oh, og,
     e, h, fwd, perm, mask, inv, halo, halo_lo, halo_hi, p_send, p_recv, eps_t, r_first, r_second, inv_eps,
-    mode_v, mode_col, lines, solved, kept, send, recv, grad,
+    mode_v, mode_col, lines, solved, kept, send, recv, send_two, recv_two, grad,
     load_sem, halo_send_sem, halo_recv_sem, p_send_sem, p_recv_sem, send_sem, recv_sem,
 ):
     me = lax.axis_index("line")
@@ -188,11 +188,11 @@
 
     barrier = pltpu.get_barrier_semaphore()
 
-    def greet(k, carry):
-        pl.semaphore_signal(barrier, inc=1, device_id={"line": lax.rem(me + k, n)}, device_id_type=MESH)
-        return carry
-
-    lax.fori_loop(1, n, greet, 0)
+    far = sorted(range(1, n), key=lambda k: -min(k, n - k))
+    turns = [k for two in zip(far, far[::-1]) for k in two][: n - 1]
+    others = [lax.rem(me + k, n) for k in turns]
+    for other in others:
+        pl.semaphore_signal(barrier, inc=1, device_id={"line": other}, device_id_type=MESH)
 
     loads = []
     for source, target in (
@@ -251,11 +251,8 @@
             device_id={"line": to}, device_id_type=MESH,
         )
 
-    def p_start(k, carry):
-        p_copy(lax.rem(me + k, n), me).start()
-        return carry
-
-    lax.fori_loop(1, n, p_start, 0)
+    for other in others:
+        p_copy(other, me).start()
     p_recv[me] = p_send[me]
 
     to_above.wait()
@@ -282,33 +279,43 @@
     for at, value in enumerate((ex, ez, h[1], e[1], hz, hx)):
         lines[at * strip : (at + 1) * strip, :] = value.astype(BF16)
 
-    def copy_out(message, to, slot):
+    groups = ((0, 2), (2, 1), (3, 1), (4, 1), (5, 1), (6, 1), (7, 2))
+
+    def copy_out(group, to, slot):
+        first, count = groups[group]
+        if count == 2:
+            out, into = (send_two.at[first // 7, to], recv_two.at[first // 7, slot])
+        else:
+            out, into = (send.at[first - 2, to], recv.at[first - 2, slot])
         return pltpu.make_async_remote_copy(
-            send.at[message, to], recv.at[message, slot], send_sem.at[message, to], recv_sem.at[message, slot],
+            out, into, send_sem.at[group, to], recv_sem.at[group, slot],
             device_id={"line": to}, device_id_type=MESH,
         )
 
-    def send_all(message):
-        def go(k, carry):
-            copy_out(message, lax.rem(me + k, n), me).start()
-            return carry
-
-        lax.fori_loop(1, n, go, 0)
-        recv[message, me] = send[message, me]
-
-    def receive_all(message):
+    def tile_at(tile, one, two, device):
+        if 2 <= tile <= 6:
+            return one.at[tile - 2, device]
+        return two.at[tile // 7, device, (tile - 7 if tile >= 7 else tile)]
+
+    def send_all(group):
+        for other in others:
+            copy_out(group, other, me).start()
+        first, count = groups[group]
+        for tile in range(first, first + count):
+            tile_at(tile, recv, recv_two, me)[...] = tile_at(tile, send, send_two, me)[...]
+
+    def receive_all(group):
         def take(k, carry):
             other = lax.rem(me + k, n)
-            copy_out(message, other, other).wait_recv()
+            copy_out(group, other, other).wait_recv()
             return carry
 
         lax.fori_loop(1, n, take, 0)
 
     def assemble(message, tile):
-        receive_all(message)
         at = tile * LANES
         for k in range(n // 2):
-            a, b = (recv[message, 2 * k], recv[message, 2 * k + 1])
+            a, b = [tile_at(message, recv, recv_two, 2 * k + odd)[...] for odd in range(2)]
             cut = slice(k * LANES, (k + 1) * LANES)
             lines[at : at + strip, cut] = jnp.concatenate([a[:, :strip], b[:, :strip]], 1)
             lines[at + strip : at + LANES, cut] = jnp.concatenate([a[:, strip:], b[:, strip:]], 1)
@@ -321,7 +328,8 @@
 
     def put(message, start, tile):
         for part in range(rows // strip):
-            send[message, start // strip + part] = tile[part * strip : (part + 1) * strip].astype(BF16)
+            target = tile_at(message, send, send_two, start // strip + part)
+            target[...] = tile[part * strip : (part + 1) * strip].astype(BF16)
 
     def swap(tile):
         return pltpu.roll(tile, LANES // 2, 1)
@@ -388,8 +396,8 @@
         put(0, start, jnp.where(low, a, swap(c)))
         put(1, start, jnp.where(low, swap(a), c))
         put(2, start, b)
-    for message in range(3):
-        send_all(message)
+    send_all(0)
+    send_all(1)
 
     def p_take(k, carry):
         other = lax.rem(me + k, n)
@@ -408,6 +416,7 @@
     loads[5].wait()
     loads[6].wait()
 
+    receive_all(0)
     assemble(0, 0)
     solve_tile(0)
     for start in starts:
@@ -421,13 +430,14 @@
         a = kept[start : start + rows, :]
         put(3, start, jnp.where(low, a, swap(b)))
         put(5, start, jnp.where(low, swap(a), b))
-    send_all(3)
+    send_all(2)
+    receive_all(1)
     assemble(2, 2)
     solve_tile(2)
     for start in starts:
         put(4, start, solved[2, start + PAD : start + PAD + rows, :])
+    send_all(3)
     send_all(4)
-    send_all(5)
 
     weight = mask[...].astype(F32)
     square = inv_eps[...] * inv_eps[...]
@@ -439,24 +449,27 @@
     grad[...] = weight * along(parts, 0) * square
 
     for tile in range(2):
+        receive_all(2 + tile)
         assemble(3 + tile, tile)
         solve_tile(tile)
     for start in starts:
         put(6, start, curl_x_first(start))
-    send_all(6)
+    send_all(5)
+    receive_all(4)
     assemble(5, 2)
     solve_tile(2)
     for start in starts:
         b, c = curl_x_second(start)
         put(7, start, b)
         put(8, start, c)
-    send_all(7)
-    send_all(8)
-
+    send_all(6)
+
+    receive_all(5)
     assemble(6, 0)
     pair = contract(lines[0:LANES, :], inv[...])
     oe[0, 0] = pair[:strip]
     oe[2, 0] = pair[strip:]
+    receive_all(6)
     assemble(7, 1)
     pair = contract(lines[LANES : 2 * LANES, :], inv[...])
     oh[1, 0] = pair[:strip]
@@ -470,8 +483,8 @@
     def settle(k, carry):
         other = lax.rem(me + k, n)
         p_copy(other, other).wait_send()
-        for message in range(9):
-            copy_out(message, other, other).wait_send()
+        for group in range(len(groups)):
+            copy_out(group, other, other).wait_send()
         return carry
 
     lax.fori_loop(1, n, settle, 0)
@@ -517,16 +530,18 @@
         pltpu.VMEM((6 * strip, cells), BF16),
         pltpu.VMEM((3, cells + 2 * PAD, LANES), F32),
         pltpu.VMEM((cells, LANES), F32),
-        pltpu.VMEM((9, n, strip, LANES), BF16),
-        pltpu.VMEM((9, n, strip, LANES), BF16),
+        pltpu.VMEM((5, n, strip, LANES), BF16),
+        pltpu.VMEM((5, n, strip, LANES), BF16),
+        pltpu.VMEM((2, n, 2, strip, LANES), BF16),
+        pltpu.VMEM((2, n, 2, strip, LANES), BF16),
         pltpu.VMEM((strip, cells), F32),
         pltpu.SemaphoreType.DMA((7,)),
         pltpu.SemaphoreType.DMA((2,)),
         pltpu.SemaphoreType.DMA((2,)),
         pltpu.SemaphoreType.DMA((n,)),
         pltpu.SemaphoreType.DMA((n,)),
-        pltpu.SemaphoreType.DMA((9, n)),
-        pltpu.SemaphoreType.DMA((9, n)),
+        pltpu.SemaphoreType.DMA((7, n)),
+        pltpu.SemaphoreType.DMA((7, n)),
     ]
     shapes = tuple(jax.ShapeDtypeStruct(a.shape, F32) for a in (adj_e, adj_h, permittivity))
     results = pl.pallas_call(
@@ -549,6 +564,7 @@
             in_specs=[pl.BlockSpec(memory_space=pl.ANY)] * 3,
             out_specs=(hbm, hbm, hbm),
             scratch_shapes=[pltpu.SemaphoreType.DMA((7,))],
+            compiler_params=pltpu.CompilerParams(vmem_limit_bytes=1024 * 1024),
         )(*results)
     )
 

time: 132 us -> 74.2 us (0.56)
  Pallas kernels: 128 us -> 72.1 us
  local copies, waits for them, and re-layouts: 2.47 us -> 0 us
    pallas_call x1, Pallas kernels: 56.7 us -> 1.28 us  [fused(): pl.pallas_call(write_out, out_shape=shapes, in_specs=[pl.BlockSpec(memory...]
    unnamed x6 -> x0, local copies, waits for them, and re-layouts: 2.47 us -> none
where the time goes in v3:
time: 74.2 us; the launch traced here: 74.1 us
  Pallas kernels  72.1 us (97%)
  between operations  1.93 us (3%)
    pallas_call x1, Pallas kernels, fused(): pl.pallas_call(functools.partial(kernel, n), out_shape=tuple((pltpu.VMEM(...  70.8 us

profile of v3, /device:TPU:0, one launch (start us, length us, event | category | flops | bytes accessed | tf_op | source)
XLA Modules:
  0.0 74.1 jit_solution(1315409038279999640)
XLA Ops:
  1.9 70.8 %shard_map.112 = (f32[3,1,64,1024]{3,2,1,0:T(8,128)S(1)}, f32[3,1,64,1024]{3,2,1,0:T(8,128)S(1)}, f32[1,64,1024]{2,1,0:T(8,128)S(1)}) custom-call(f32[3,1,64,1024]{3,2,1,0:T(8,128)} %e_hbm.1, f32[3,1,64,1024]{3,2,1,0:T(8,128)} %h_hbm.1, bf16[2,3,1,64,1024]{4,3,2,1,0:T(8,128)(2,1)} %fwd_hbm.1, f32[1,64,1024]{2,1,0:T(8,128)} %perm_hbm.1, ...), custom_call_target="tpu_custom_call" | custom-call | tf_op jit(solution)/shard_map/pallas_call | solution.py:547
  72.8 1.3 %shard_map.113 = (f32[3,1,64,1024]{3,2,1,0:T(8,128)}, f32[3,1,64,1024]{3,2,1,0:T(8,128)}, f32[1,64,1024]{2,1,0:T(8,128)}) custom-call(f32[3,1,64,1024]{3,2,1,0:T(8,128)S(1)} %get-tuple-element.6.e, f32[3,1,64,1024]{3,2,1,0:T(8,128)S(1)} %get-tuple-element.7.h, f32[1,64,1024]{2,1,0:T(8,128)S(1)} %get-tuple-element.8.g), custom_call_target="tpu_custom_call" | custom-call | tf_op jit(solution)/shard_map/pallas_call | solution.py:561

commit v4 on v3

--- a/solution.py
+++ b/solution.py
@@ -156,6 +156,7 @@
 LANES = 128
 MESH = pl.DeviceIdType.MESH
 PAD = 8
+EDGE = 16
 F32, BF16 = (jnp.float32, jnp.bfloat16)
 
 
@@ -179,11 +180,13 @@
     oe, oh, og,
     e, h, fwd, perm, mask, inv, halo, halo_lo, halo_hi, p_send, p_recv, eps_t, r_first, r_second, inv_eps,
     mode_v, mode_col, lines, solved, kept, send, recv, send_two, recv_two, grad,
-    load_sem, halo_send_sem, halo_recv_sem, p_send_sem, p_recv_sem, send_sem, recv_sem,
+    load_sem, hand_sem, halo_send_sem, halo_recv_sem, p_send_sem, p_recv_sem, send_sem, recv_sem,
 ):
-    me = lax.axis_index("line")
+    me, core = (lax.axis_index("line"), lax.axis_index("exc"))
     strip = perm.shape[0]
-    cells = inv.shape[0]
+    cells = perm.shape[1]
+    half = strip // 4
+    inverse = inv.at[EDGE : cells + EDGE]
     above, below = (lax.rem(me + 1, n), lax.rem(me + n - 1, n))
 
     barrier = pltpu.get_barrier_semaphore()
@@ -194,9 +197,11 @@
     for other in others:
         pl.semaphore_signal(barrier, inc=1, device_id={"line": other}, device_id_type=MESH)
 
+    pl.semaphore_signal(barrier, inc=1, device_id={"exc": 1 - core}, device_id_type=MESH)
+
     loads = []
     for source, target in (
-        (perm_hbm.at[0], perm), (mode_hbm, mode_v), (e_hbm.at[:, 0], e), (h_hbm.at[:, 0], h), (inv_hbm, inv),
+        (perm_hbm.at[0], perm), (mode_hbm, mode_v), (e_hbm.at[:, 0], e), (h_hbm.at[:, 0], h), (inv_hbm, inverse),
         (fwd_hbm.at[:, :, 0], fwd), (mask_hbm.at[0], mask),
     ):
         copy = pltpu.make_async_copy(source, target, load_sem.at[len(loads)])
@@ -234,7 +239,7 @@
         0,
     )
 
-    pl.semaphore_wait(barrier, n - 1)
+    pl.semaphore_wait(barrier, n)
 
     to_above = pltpu.make_async_remote_copy(
         halo, halo_lo, halo_send_sem.at[0], halo_recv_sem.at[0], device_id={"line": above}, device_id_type=MESH
@@ -247,13 +252,13 @@
 
     def p_copy(to, slot):
         return pltpu.make_async_remote_copy(
-            p_send.at[to], p_recv.at[slot], p_send_sem.at[to], p_recv_sem.at[slot],
+            p_send.at[to, pl.ds(pl.multiple_of(core * half, half), half)], p_recv.at[core, slot], p_send_sem.at[to], p_recv_sem.at[slot],
             device_id={"line": to}, device_id_type=MESH,
         )
 
     for other in others:
         p_copy(other, me).start()
-    p_recv[me] = p_send[me]
+    p_recv[core, me] = p_send[me, pl.ds(pl.multiple_of(core * half, half), half), :]
 
     to_above.wait()
     to_below.wait()
@@ -300,6 +305,9 @@
     def send_all(group):
         for other in others:
             copy_out(group, other, me).start()
+        keep_own(group)
+
+    def keep_own(group):
         first, count = groups[group]
         for tile in range(first, first + count):
             tile_at(tile, recv, recv_two, me)[...] = tile_at(tile, send, send_two, me)[...]
@@ -322,20 +330,20 @@
 
     def solve_tile(tile):
         part = lines[tile * LANES : (tile + 1) * LANES, :]
-        solved[tile, PAD : cells + PAD, :] = contract(inv[...], part)
+        solved[tile, PAD : cells + PAD, :] = contract(inverse[...], part)
 
     rows = LANES
 
-    def put(message, start, tile):
+    def put(message, device, tile):
         for part in range(rows // strip):
-            target = tile_at(message, send, send_two, start // strip + part)
+            target = tile_at(message, send, send_two, device + part)
             target[...] = tile[part * strip : (part + 1) * strip].astype(BF16)
 
     def swap(tile):
         return pltpu.roll(tile, LANES // 2, 1)
 
-    def extended(tile, start, back):
-        return solved[tile, start + PAD - back : start + PAD - back + rows + PAD, :]
+    def extended(tile, off, back):
+        return solved[tile, off - back : off - back + rows + PAD, :]
 
     def next_row(value):
         return pltpu.roll(value, value.shape[0] - 1, 0)
@@ -343,27 +351,26 @@
     def in_grid(start):
         return lax.broadcasted_iota(jnp.int32, (rows + PAD, LANES), 0) + start < cells
 
-    def curl_x_first(start):
-        here = slice(start + PAD, start + PAD + rows)
-        b, bd = (solved[1, here, :], solved[1, start + PAD - 1 : start + PAD - 1 + rows, :])
+    def curl_x_first(off, at, count):
+        b, bd = (solved[1, off : off + count, :], solved[1, off - 1 : off - 1 + count, :])
         hy, hyd = (jnp.where(low, b, swap(b)), jnp.where(low, bd, swap(bd)))
-        a = solved[0, here, :] + r_first[start : start + rows, :] * jnp.where(low, -hy, hy - hyd)
-        solved[0, here, :] = a
+        a = solved[0, off : off + count, :] + r_first[pl.ds(at, count), :] * jnp.where(low, -hy, hy - hyd)
+        solved[0, off : off + count, :] = a
         return a
 
-    def curl_x_second(start):
-        a, b, c = (extended(0, start, 0), extended(1, start, 0), extended(2, start, 0))
+    def curl_x_second(off, at):
+        a, b, c = (extended(0, off, 0), extended(1, off, 0), extended(2, off, 0))
         sa, sc = (swap(a), swap(c))
-        dc = sc - swap(extended(2, start, 1))
-        ey = b + r_first[start : start + rows + PAD, :] * (c - dc)
-        ey = jnp.where(in_grid(start), ey, 0.0)
+        dc = sc - swap(extended(2, off, 1))
+        ey = b + r_first[pl.ds(at, rows + PAD), :] * (c - dc)
+        ey = jnp.where(in_grid(at), ey, 0.0)
         hy = b + COURANT * ((next_row(sa) - sa) + a)
         sy = swap(ey)
         c = c - COURANT * jnp.where(low, next_row(sy) - sy, ey)
         return jnp.where(low, hy, ey)[0:rows], c[0:rows]
 
     def curl_y(tile, start, sign, source):
-        t, td = (extended(tile, start, 0), extended(tile, start, 1))
+        t, td = (extended(tile, start + PAD, 0), extended(tile, start + PAD, 1))
         st, std = (swap(t), swap(td))
         p = t if source is None else t + source
         p = p + sign * r_second[start : start + rows + PAD, :] * (st - std)
@@ -379,25 +386,37 @@
             + electric[2] * fwd[instant, 2].astype(F32)
         )
 
+    starts = range(0, cells, rows)
+
+    loads[4].wait()
+    inv[0:EDGE, :] = jnp.zeros((EDGE, cells), BF16)
+    inv[cells + EDGE :, :] = jnp.zeros((EDGE, cells), BF16)
+    quarter, group = (cells // 4, n // 4)
+    for turn in (2, 3, 1, 0):
+        plane_of = lax.rem(me // group + turn, 4)
+        at = pl.multiple_of(plane_of * quarter, quarter)
+        result = contract(inv[pl.ds(at, quarter + 2 * EDGE), :], lines[...])
+        for tile in range(3):
+            solved[tile, 0 : quarter + 2 * EDGE, :] = result[:, tile * LANES : (tile + 1) * LANES]
+        for part in range(0, quarter, rows):
+            curl_x_first(EDGE + part, pl.multiple_of(at + part, rows), rows)
+        curl_x_first(EDGE + quarter, pl.multiple_of(at + quarter, rows), PAD)
+        for part in range(0, quarter, rows):
+            b, c = curl_x_second(EDGE + part, pl.multiple_of(at + part, rows))
+            a = solved[0, EDGE + part : EDGE + part + rows, :]
+            device = plane_of * group + part // strip
+            put(0, device, jnp.where(low, a, swap(c)))
+            put(1, device, jnp.where(low, swap(a), c))
+            put(2, device, b)
+        for k in range(1 if turn == 0 else 0, group):
+            other = plane_of * group + lax.rem(lax.rem(me, group) + k, group)
+            copy_out(0, other, me).start()
+    keep_own(0)
+    send_all(1)
+
     for tile in range(3):
         solved[tile, 0:PAD, :] = jnp.zeros((PAD, LANES), F32)
         solved[tile, cells + PAD :, :] = jnp.zeros((PAD, LANES), F32)
-    starts = range(0, cells, rows)
-
-    loads[4].wait()
-    result = contract(inv[...], lines[...])
-    for tile in range(3):
-        solved[tile, PAD : cells + PAD, :] = result[:, tile * LANES : (tile + 1) * LANES]
-    for start in starts:
-        curl_x_first(start)
-    for start in starts:
-        a = solved[0, start + PAD : start + PAD + rows, :]
-        b, c = curl_x_second(start)
-        put(0, start, jnp.where(low, a, swap(c)))
-        put(1, start, jnp.where(low, swap(a), c))
-        put(2, start, b)
-    send_all(0)
-    send_all(1)
 
     def p_take(k, carry):
         other = lax.rem(me + k, n)
@@ -405,11 +424,19 @@
         return carry
 
     lax.fori_loop(1, n, p_take, 0)
+    hand_over = pltpu.make_async_remote_copy(
+        p_recv.at[core], p_recv.at[core], hand_sem.at[0], hand_sem.at[1],
+        device_id={"exc": 1 - core}, device_id_type=MESH,
+    )
+    hand_over.start()
+    hand_over.wait()
     for k in range(n // 2):
-        a, b = (p_recv[2 * k], p_recv[2 * k + 1])
         cut = slice(k * LANES, (k + 1) * LANES)
-        inv_eps[0 : strip // 2, cut] = 1.0 / jnp.concatenate([a[:, :strip], b[:, :strip]], 1)
-        inv_eps[strip // 2 :, cut] = 1.0 / jnp.concatenate([a[:, strip:], b[:, strip:]], 1)
+        for part in range(2):
+            a, b = (p_recv[part, 2 * k], p_recv[part, 2 * k + 1])
+            one, two = (part * half, part * half + strip // 2)
+            inv_eps[one : one + half, cut] = 1.0 / jnp.concatenate([a[:, :strip], b[:, :strip]], 1)
+            inv_eps[two : two + half, cut] = 1.0 / jnp.concatenate([a[:, strip:], b[:, strip:]], 1)
     both = jnp.concatenate([inv_eps[...], inv_eps[...]], 0)
     r_second[0:cells, :] = COURANT * both.T
     r_second[cells:, :] = jnp.zeros((PAD, LANES), F32)
@@ -428,14 +455,14 @@
         source = (amplitudes[1] * mode_col[start : start + rows + PAD, :]) * here
         b = curl_y(1, start, -1.0, source)
         a = kept[start : start + rows, :]
-        put(3, start, jnp.where(low, a, swap(b)))
-        put(5, start, jnp.where(low, swap(a), b))
+        put(3, start // strip, jnp.where(low, a, swap(b)))
+        put(5, start // strip, jnp.where(low, swap(a), b))
     send_all(2)
     receive_all(1)
     assemble(2, 2)
     solve_tile(2)
     for start in starts:
-        put(4, start, solved[2, start + PAD : start + PAD + rows, :])
+        put(4, start // strip, solved[2, start + PAD : start + PAD + rows, :])
     send_all(3)
     send_all(4)
 
@@ -444,7 +471,7 @@
     electric = jnp.concatenate(
         [lines[0:strip, :], lines[LANES + strip * 0 : LANES + strip, :], lines[2 * LANES + strip :, :]], 0
     )
-    electric = contract(electric, inv[...])
+    electric = contract(electric, inverse[...])
     parts = (electric[0:strip], electric[2 * strip :], electric[strip : 2 * strip])
     grad[...] = weight * along(parts, 0) * square
 
@@ -453,30 +480,30 @@
         assemble(3 + tile, tile)
         solve_tile(tile)
     for start in starts:
-        put(6, start, curl_x_first(start))
+        put(6, start // strip, curl_x_first(start + PAD, start, rows))
     send_all(5)
     receive_all(4)
     assemble(5, 2)
     solve_tile(2)
     for start in starts:
-        b, c = curl_x_second(start)
-        put(7, start, b)
-        put(8, start, c)
+        b, c = curl_x_second(start + PAD, start)
+        put(7, start // strip, b)
+        put(8, start // strip, c)
     send_all(6)
 
     receive_all(5)
     assemble(6, 0)
-    pair = contract(lines[0:LANES, :], inv[...])
+    pair = contract(lines[0:LANES, :], inverse[...])
     oe[0, 0] = pair[:strip]
     oe[2, 0] = pair[strip:]
     receive_all(6)
     assemble(7, 1)
-    pair = contract(lines[LANES : 2 * LANES, :], inv[...])
+    pair = contract(lines[LANES : 2 * LANES, :], inverse[...])
     oh[1, 0] = pair[:strip]
     oe[1, 0] = pair[strip:]
     og[0] = grad[...] + weight * along((oe[0, 0], pair[strip:], oe[2, 0]), 1) * square
     assemble(8, 2)
-    pair = contract(lines[2 * LANES :, :], inv[...])
+    pair = contract(lines[2 * LANES :, :], inverse[...])
     oh[2, 0] = pair[:strip]
     oh[0, 0] = pair[strip:]
 
@@ -515,12 +542,12 @@
         pltpu.VMEM((steps, 3, strip, cells), BF16),
         pltpu.VMEM((strip, cells), F32),
         pltpu.VMEM((strip, cells), jnp.int32),
-        pltpu.VMEM((cells, cells), BF16),
+        pltpu.VMEM((cells + 2 * EDGE, cells), BF16),
         pltpu.VMEM((8, cells), F32),
         pltpu.VMEM((8, cells), F32),
         pltpu.VMEM((8, cells), F32),
         pltpu.VMEM((n, strip // 2, LANES), F32),
-        pltpu.VMEM((n, strip // 2, LANES), F32),
+        pltpu.VMEM((2, n, strip // 4, LANES), F32),
         pltpu.VMEM((cells, LANES), F32),
         pltpu.VMEM((cells + PAD, LANES), F32),
         pltpu.VMEM((cells + PAD, LANES), F32),
@@ -536,6 +563,7 @@
         pltpu.VMEM((2, n, 2, strip, LANES), BF16),
         pltpu.VMEM((strip, cells), F32),
         pltpu.SemaphoreType.DMA((7,)),
+        pltpu.SemaphoreType.DMA((2,)),
         pltpu.SemaphoreType.DMA((2,)),
         pltpu.SemaphoreType.DMA((2,)),
         pltpu.SemaphoreType.DMA((n,)),
@@ -571,7 +599,7 @@
 
 def per_device(adj_e, adj_h, fwd_e, permittivity, design_mask, inverse, omega, port_mode, port_plane):
     args = (adj_e, adj_h, fwd_e, permittivity, design_mask, inverse, omega, port_mode, port_plane)
-    paired = 2 * adj_e.shape[2] == LANES and fwd_e.shape[0] == 2 and permittivity.shape[0] == 1
+    paired = 2 * adj_e.shape[2] == LANES and fwd_e.shape[0] == 2 and lax.axis_size("exc") == 2 and permittivity.shape[0] == 1
     return fused(*args) if paired else plain_per_device(*args)
 
 

time: 74.2 us -> 71.3 us (0.961)
  Pallas kernels: 72.1 us -> 69.2 us
    pallas_call x1, Pallas kernels: 70.8 us -> 67.9 us  [fused(): pl.pallas_call(functools.partial(kernel, n), out_shape=tuple((pltpu.VMEM(...]
where the time goes in v4:
time: 71.3 us; the launch traced here: 71.2 us
  Pallas kernels  69.2 us (97%)
  between operations  1.93 us (3%)
    pallas_call x1, Pallas kernels, fused(): pl.pallas_call(functools.partial(kernel, n), out_shape=tuple((pltpu.VMEM(...  67.9 us

profile of v4, /device:TPU:0, one launch (start us, length us, event | category | flops | bytes accessed | tf_op | source)
XLA Modules:
  0.0 71.2 jit_solution(8166422099429218888)
XLA Ops:
  1.9 67.9 %shard_map.112 = (f32[3,1,64,1024]{3,2,1,0:T(8,128)S(1)}, f32[3,1,64,1024]{3,2,1,0:T(8,128)S(1)}, f32[1,64,1024]{2,1,0:T(8,128)S(1)}) custom-call(f32[3,1,64,1024]{3,2,1,0:T(8,128)} %e_hbm.1, f32[3,1,64,1024]{3,2,1,0:T(8,128)} %h_hbm.1, bf16[2,3,1,64,1024]{4,3,2,1,0:T(8,128)(2,1)} %fwd_hbm.1, f32[1,64,1024]{2,1,0:T(8,128)} %perm_hbm.1, ...), custom_call_target="tpu_custom_call" | custom-call | tf_op jit(solution)/shard_map/pallas_call | solution.py:575
  69.9 1.3 %shard_map.113 = (f32[3,1,64,1024]{3,2,1,0:T(8,128)}, f32[3,1,64,1024]{3,2,1,0:T(8,128)}, f32[1,64,1024]{2,1,0:T(8,128)}) custom-call(f32[3,1,64,1024]{3,2,1,0:T(8,128)S(1)} %get-tuple-element.6.e, f32[3,1,64,1024]{3,2,1,0:T(8,128)S(1)} %get-tuple-element.7.h, f32[1,64,1024]{2,1,0:T(8,128)S(1)} %get-tuple-element.8.g), custom_call_target="tpu_custom_call" | custom-call | tf_op jit(solution)/shard_map/pallas_call | solution.py:589

commit v5 on v4

--- a/solution.py
+++ b/solution.py
@@ -201,7 +201,7 @@
 
     loads = []
     for source, target in (
-        (perm_hbm.at[0], perm), (mode_hbm, mode_v), (e_hbm.at[:, 0], e), (h_hbm.at[:, 0], h), (inv_hbm, inverse),
+        (e_hbm.at[:, 0], e), (h_hbm.at[:, 0], h), (perm_hbm.at[0], perm), (mode_hbm, mode_v), (inv_hbm, inverse),
         (fwd_hbm.at[:, :, 0], fwd), (mask_hbm.at[0], mask),
     ):
         copy = pltpu.make_async_copy(source, target, load_sem.at[len(loads)])
@@ -211,17 +211,47 @@
     lane = lax.broadcasted_iota(jnp.int32, (1, LANES), 1)
     low = lane < strip
 
-    loads[0].wait()
+    for load in loads[:3]:
+        load.wait()
+    halo[...] = jnp.concatenate(
+        [
+            e[0, 0:1, :], e[2, 0:1, :], h[0, 0:1, :], h[2, 0:1, :], perm[0:1, :],
+            h[0, strip - 1 : strip, :], h[2, strip - 1 : strip, :], perm[0:1, :],
+        ],
+        0,
+    )
+
+    pl.semaphore_wait(barrier, n)
+
+    to_above = pltpu.make_async_remote_copy(
+        halo, halo_lo, halo_send_sem.at[0], halo_recv_sem.at[0], device_id={"line": above}, device_id_type=MESH
+    )
+    to_below = pltpu.make_async_remote_copy(
+        halo, halo_hi, halo_send_sem.at[1], halo_recv_sem.at[1], device_id={"line": below}, device_id_type=MESH
+    )
+    to_above.start()
+    to_below.start()
+
     twice = jnp.concatenate([perm[...], perm[...]], 0)
     eps_t[...] = twice.T
     for block in range(n):
         first = eps_t[block * strip : block * strip + strip // 2, :]
         second = eps_t[block * strip + strip // 2 : (block + 1) * strip, :]
         p_send[block] = jnp.where(low, first, second)
+    def p_copy(to, slot):
+        return pltpu.make_async_remote_copy(
+            p_send.at[to, pl.ds(pl.multiple_of(core * half, half), half)], p_recv.at[core, slot], p_send_sem.at[to], p_recv_sem.at[slot],
+            device_id={"line": to}, device_id_type=MESH,
+        )
+
+    for other in others:
+        p_copy(other, me).start()
+    p_recv[core, me] = p_send[me, pl.ds(pl.multiple_of(core * half, half), half), :]
+
     r_first[0:cells, :] = COURANT * (1.0 / eps_t[...])
     r_first[cells:, :] = jnp.zeros((PAD, LANES), F32)
 
-    loads[1].wait()
+    loads[3].wait()
     for block in range(cells // LANES):
         line = jnp.broadcast_to(mode_v[block : block + 1, :], (LANES, LANES))
         mode_col[block * LANES : (block + 1) * LANES, :] = line.T
@@ -229,39 +259,6 @@
     amplitudes = [jnp.cos(jnp.full((1, LANES), omega[0] * (s + 1), F32)) for s in range(2)]
     at_plane = plane[0]
 
-    loads[2].wait()
-    loads[3].wait()
-    halo[...] = jnp.concatenate(
-        [
-            e[0, 0:1, :], e[2, 0:1, :], h[0, 0:1, :], h[2, 0:1, :], perm[0:1, :],
-            h[0, strip - 1 : strip, :], h[2, strip - 1 : strip, :], perm[0:1, :],
-        ],
-        0,
-    )
-
-    pl.semaphore_wait(barrier, n)
-
-    to_above = pltpu.make_async_remote_copy(
-        halo, halo_lo, halo_send_sem.at[0], halo_recv_sem.at[0], device_id={"line": above}, device_id_type=MESH
-    )
-    to_below = pltpu.make_async_remote_copy(
-        halo, halo_hi, halo_send_sem.at[1], halo_recv_sem.at[1], device_id={"line": below}, device_id_type=MESH
-    )
-    to_above.start()
-    to_below.start()
-
-    def p_copy(to, slot):
-        return pltpu.make_async_remote_copy(
-            p_send.at[to, pl.ds(pl.multiple_of(core * half, half), half)], p_recv.at[core, slot], p_send_sem.at[to], p_recv_sem.at[slot],
-            device_id={"line": to}, device_id_type=MESH,
-        )
-
-    for other in others:
-        p_copy(other, me).start()
-    p_recv[core, me] = p_send[me, pl.ds(pl.multiple_of(core * half, half), half), :]
-
-    to_above.wait()
-    to_below.wait()
     is_first, is_last = (me == 0, me == n - 1)
     x_at = lax.broadcasted_iota(jnp.int32, (1, cells), 1)
     column = jnp.where(x_at == at_plane, 1.0, 0.0)
@@ -270,6 +267,8 @@
     source = profile * column
     r = COURANT * (1.0 / perm[...])
     ex, ez, hx, hz = (e[0], e[2] + source[0:strip], h[0], h[2])
+    to_above.wait()
+    to_below.wait()
     hx_lo = jnp.where(is_first, 0.0, halo_lo[5:6, :])
     hz_lo = jnp.where(is_first, 0.0, halo_lo[6:7, :])
     ex = ex + r * (hz - shifted_down(hz, hz_lo))
@@ -284,12 +283,12 @@
     for at, value in enumerate((ex, ez, h[1], e[1], hz, hx)):
         lines[at * strip : (at + 1) * strip, :] = value.astype(BF16)
 
-    groups = ((0, 2), (2, 1), (3, 1), (4, 1), (5, 1), (6, 1), (7, 2))
+    groups = ((0, 2), (2, 1), (3, 1), (4, 1), (5, 1), (6, 1), (7, 1), (8, 1))
 
     def copy_out(group, to, slot):
         first, count = groups[group]
         if count == 2:
-            out, into = (send_two.at[first // 7, to], recv_two.at[first // 7, slot])
+            out, into = (send_two.at[to], recv_two.at[slot])
         else:
             out, into = (send.at[first - 2, to], recv.at[first - 2, slot])
         return pltpu.make_async_remote_copy(
@@ -298,9 +297,7 @@
         )
 
     def tile_at(tile, one, two, device):
-        if 2 <= tile <= 6:
-            return one.at[tile - 2, device]
-        return two.at[tile // 7, device, (tile - 7 if tile >= 7 else tile)]
+        return two.at[device, tile] if tile < 2 else one.at[tile - 2, device]
 
     def send_all(group):
         for other in others:
@@ -490,6 +487,7 @@
         put(7, start // strip, b)
         put(8, start // strip, c)
     send_all(6)
+    send_all(7)
 
     receive_all(5)
     assemble(6, 0)
@@ -502,6 +500,7 @@
     oh[1, 0] = pair[:strip]
     oe[1, 0] = pair[strip:]
     og[0] = grad[...] + weight * along((oe[0, 0], pair[strip:], oe[2, 0]), 1) * square
+    receive_all(7)
     assemble(8, 2)
     pair = contract(lines[2 * LANES :, :], inverse[...])
     oh[2, 0] = pair[:strip]
@@ -557,10 +556,10 @@
         pltpu.VMEM((6 * strip, cells), BF16),
         pltpu.VMEM((3, cells + 2 * PAD, LANES), F32),
         pltpu.VMEM((cells, LANES), F32),
-        pltpu.VMEM((5, n, strip, LANES), BF16),
-        pltpu.VMEM((5, n, strip, LANES), BF16),
-        pltpu.VMEM((2, n, 2, strip, LANES), BF16),
-        pltpu.VMEM((2, n, 2, strip, LANES), BF16),
+        pltpu.VMEM((7, n, strip, LANES), BF16),
+        pltpu.VMEM((7, n, strip, LANES), BF16),
+        pltpu.VMEM((n, 2, strip, LANES), BF16),
+        pltpu.VMEM((n, 2, strip, LANES), BF16),
         pltpu.VMEM((strip, cells), F32),
         pltpu.SemaphoreType.DMA((7,)),
         pltpu.SemaphoreType.DMA((2,)),
@@ -568,8 +567,8 @@
         pltpu.SemaphoreType.DMA((2,)),
         pltpu.SemaphoreType.DMA((n,)),
         pltpu.SemaphoreType.DMA((n,)),
-        pltpu.SemaphoreType.DMA((7, n)),
-        pltpu.SemaphoreType.DMA((7, n)),
+        pltpu.SemaphoreType.DMA((8, n)),
+        pltpu.SemaphoreType.DMA((8, n)),
     ]
     shapes = tuple(jax.ShapeDtypeStruct(a.shape, F32) for a in (adj_e, adj_h, permittivity))
     results = pl.pallas_call(

time: 71.3 us -> 71.1 us (level)
  no operation moved by 1% of the time
where the time goes in v5:
time: 71.1 us; the launch traced here: 70.9 us
  Pallas kernels  68.8 us (97%)
  between operations  2.09 us (3%)
    pallas_call x1, Pallas kernels, fused(): pl.pallas_call(functools.partial(kernel, n), out_shape=tuple((pltpu.VMEM(...  67.6 us

profile of v5, /device:TPU:0, one launch (start us, length us, event | category | flops | bytes accessed | tf_op | source)
XLA Modules:
  0.0 70.9 jit_solution(7622732393928792689)
XLA Ops:
  1.9 67.6 %shard_map.112 = (f32[3,1,64,1024]{3,2,1,0:T(8,128)S(1)}, f32[3,1,64,1024]{3,2,1,0:T(8,128)S(1)}, f32[1,64,1024]{2,1,0:T(8,128)S(1)}) custom-call(f32[3,1,64,1024]{3,2,1,0:T(8,128)} %e_hbm.1, f32[3,1,64,1024]{3,2,1,0:T(8,128)} %h_hbm.1, bf16[2,3,1,64,1024]{4,3,2,1,0:T(8,128)(2,1)} %fwd_hbm.1, f32[1,64,1024]{2,1,0:T(8,128)} %perm_hbm.1, ...), custom_call_target="tpu_custom_call" | custom-call | tf_op jit(solution)/shard_map/pallas_call | solution.py:574
  69.5 1.3 %shard_map.113 = (f32[3,1,64,1024]{3,2,1,0:T(8,128)}, f32[3,1,64,1024]{3,2,1,0:T(8,128)}, f32[1,64,1024]{2,1,0:T(8,128)}) custom-call(f32[3,1,64,1024]{3,2,1,0:T(8,128)S(1)} %get-tuple-element.6.e, f32[3,1,64,1024]{3,2,1,0:T(8,128)S(1)} %get-tuple-element.7.h, f32[1,64,1024]{2,1,0:T(8,128)S(1)} %get-tuple-element.8.g), custom_call_target="tpu_custom_call" | custom-call | tf_op jit(solution)/shard_map/pallas_call | solution.py:588

commit v6 on v5

--- a/solution.py
+++ b/solution.py
@@ -191,8 +191,7 @@
 
     barrier = pltpu.get_barrier_semaphore()
 
-    far = sorted(range(1, n), key=lambda k: -min(k, n - k))
-    turns = [k for two in zip(far, far[::-1]) for k in two][: n - 1]
+    turns = sorted(range(1, n), key=lambda k: -min(k, n - k))
     others = [lax.rem(me + k, n) for k in turns]
     for other in others:
         pl.semaphore_signal(barrier, inc=1, device_id={"line": other}, device_id_type=MESH)

time: 71.1 us -> 71.2 us (level)
  no operation moved by 1% of the time
where the time goes in v6:
time: 71.2 us; the launch traced here: 71.1 us
  Pallas kernels  69 us (97%)
  between operations  2.09 us (3%)
    pallas_call x1, Pallas kernels, fused(): pl.pallas_call(functools.partial(kernel, n), out_shape=tuple((pltpu.VMEM(...  67.7 us

profile of v6, /device:TPU:0, one launch (start us, length us, event | category | flops | bytes accessed | tf_op | source)
XLA Modules:
  0.0 71.1 jit_solution(320978026421431137)
XLA Ops:
  1.9 67.7 %shard_map.112 = (f32[3,1,64,1024]{3,2,1,0:T(8,128)S(1)}, f32[3,1,64,1024]{3,2,1,0:T(8,128)S(1)}, f32[1,64,1024]{2,1,0:T(8,128)S(1)}) custom-call(f32[3,1,64,1024]{3,2,1,0:T(8,128)} %e_hbm.1, f32[3,1,64,1024]{3,2,1,0:T(8,128)} %h_hbm.1, bf16[2,3,1,64,1024]{4,3,2,1,0:T(8,128)(2,1)} %fwd_hbm.1, f32[1,64,1024]{2,1,0:T(8,128)} %perm_hbm.1, ...), custom_call_target="tpu_custom_call" | custom-call | tf_op jit(solution)/shard_map/pallas_call | solution.py:573
  69.6 1.3 %shard_map.113 = (f32[3,1,64,1024]{3,2,1,0:T(8,128)}, f32[3,1,64,1024]{3,2,1,0:T(8,128)}, f32[1,64,1024]{2,1,0:T(8,128)}) custom-call(f32[3,1,64,1024]{3,2,1,0:T(8,128)S(1)} %get-tuple-element.6.e, f32[3,1,64,1024]{3,2,1,0:T(8,128)S(1)} %get-tuple-element.7.h, f32[1,64,1024]{2,1,0:T(8,128)S(1)} %get-tuple-element.8.g), custom_call_target="tpu_custom_call" | custom-call | tf_op jit(solution)/shard_map/pallas_call | solution.py:587
